TPU v7x, 128 devices: a whole 4x4x4 slice. The times are simulated.
128 devices in a mesh: lat: 8 (over y, core), lon: 16 (over x, z).
Axes of the slice: x: 4, y: 4, z: 4, core: 2. Of those that a mesh axis runs over, the one named last changes fastest.
Arguments:
- node_states: bfloat16 [65536, 512], P(('lat', 'lon')), may hold values from -6 to 6
- edge_states: bfloat16 [262144, 512], P(('lat', 'lon')), may hold values from -6 to 6
- senders: int32 [262144], P(('lat', 'lon')), may hold values from 0 to 767, as said below
- receivers: int32 [262144], P(('lat', 'lon')), may hold values from 0 to 511
- live_count: int32 [128], P(('lat', 'lon')), may hold values from 256 to 2048, as said below
- send_rows: int32 [128, 256], P(('lat', 'lon')), may hold values from 0 to 511
- node_cotangent: bfloat16 [65536, 512], P(('lat', 'lon')), may hold values from -6 to 6
- edge_inner: bfloat16 [1536, 512], replicated, may hold values from -0.15625 to 0.15625
- edge_inbias: float32 [512], replicated, may hold values from -3 to 3
- edge_outer: bfloat16 [512, 512], replicated, may hold values from -0.25 to 0.25
- edge_outbias: float32 [512], replicated, may hold values from -3 to 3
- edge_gain: float32 [512], replicated, may hold values from 0.1 to 1.9
- node_inner: bfloat16 [1024, 512], replicated, may hold values from -0.1875 to 0.1875
- node_inbias: float32 [512], replicated, may hold values from -3 to 3
- node_outer: bfloat16 [512, 512], replicated, may hold values from -0.25 to 0.25
- node_outbias: float32 [512], replicated, may hold values from -3 to 3
- node_gain: float32 [512], replicated, may hold values from 0.1 to 1.9
Outputs:
- new_nodes: bfloat16 [65536, 512], P(('lat', 'lon'))
- node_grad: bfloat16 [65536, 512], P(('lat', 'lon'))
- edge_grad: bfloat16 [262144, 512], P(('lat', 'lon'))
- edge_inner_grad: float32 [1536, 512], replicated
- edge_inbias_grad: float32 [512], replicated
- edge_outer_grad: float32 [512, 512], replicated
- edge_outbias_grad: float32 [512], replicated
- edge_gain_grad: float32 [512], replicated
- node_inner_grad: float32 [1024, 512], replicated
- node_inbias_grad: float32 [512], replicated
- node_outer_grad: float32 [512, 512], replicated
- node_outbias_grad: float32 [512], replicated
- node_gain_grad: float32 [512], replicated
Inputs may be any that keep to these rules, and one draw needn't show every extreme that they name: `senders`: below 512 an edge's sender is a node of its own patch; 512 + n * 32 + s names the s-th row that its neighbour n sends to it. No edge names a neighbour beyond the first or last lat index. Both ends of the range occur. `live_count`: edge rows of a patch past this count are padding; some patch has all 2048 rows live. send_rows[p, n * 32 + s] is a node of patch p that it sends to its neighbour n; rows may repeat.
All inputs are finite; a program needn't handle non-finite values.
Results may differ from a plain program's by a relative error of at most 0.015.
Values may be sent and summed in bfloat16 or wider, within the bound.
A program may use at most 192 MiB of HBM per device.

v0:
```python
import functools

import jax
import jax.numpy as jnp
from jax import lax
from jax.experimental import pallas as pl
from jax.experimental.pallas import tpu as pltpu
from jax.sharding import PartitionSpec as P

MESH = pl.DeviceIdType.MESH
F32 = jnp.float32
BF16 = jnp.bfloat16
I32 = jnp.int32
epsilon = 1e-05

D = 512
NODE = 512
EDGE = 2048
SLOT = 32
PEER = 256
TABLE = NODE + PEER
WIDE = TABLE + NODE
CHUNK = 512
STEPS = EDGE // CHUNK
LANE = 128
N_LAT = 8
N_LON = 16
OFFSETS = ((-1, -1), (-1, 0), (-1, 1), (0, -1), (0, 1), (1, -1), (1, 0), (1, 1))


def dot(a, b):
    return jnp.dot(a, b, preferred_element_type=F32)


def dot_rt(a, b):
    return lax.dot_general(a, b, (((1,), (1,)), ((), ())), preferred_element_type=F32)


def dot_lt(a, b):
    return lax.dot_general(a, b, (((0,), (0,)), ((), ())), preferred_element_type=F32)


def row_mean(x):
    return jnp.sum(x, axis=-1, keepdims=True) * (1.0 / D)


def col_sum(x):
    return jnp.sum(x, axis=0, keepdims=True)


def silu_parts(z):
    sig = 0.5 + 0.5 * jnp.tanh(0.5 * z)
    h = z * sig
    return h, sig + h * (1.0 - sig)


def normalize(post):
    centered = post - row_mean(post)
    scale = lax.rsqrt(row_mean(centered * centered) + epsilon)
    return centered * scale, scale


def norm_back(t, normed, scale):
    return scale * (t - row_mean(t) - normed * row_mean(t * normed))


def column_of(row):
    return jnp.transpose(jnp.broadcast_to(row.astype(F32), (LANE, LANE))).astype(I32)


def lanes(base):
    return lax.broadcasted_iota(I32, (LANE, LANE), 1) + base


def hot(mask):
    return jnp.where(mask, 1.0, 0.0).astype(BF16)


class Place:
    def __init__(self):
        self.lat = lax.axis_index("lat")
        self.lon = lax.axis_index("lon")
        self.core = lax.rem(self.lat, 2)
        self.y = lax.div(self.lat, 2)
        self.x = lax.div(self.lon, 4)
        self.z = lax.rem(self.lon, 4)

    def neighbour(self, n):
        dlat, dlon = OFFSETS[n]
        return (
            lax.rem(self.lat + (dlat + N_LAT), N_LAT),
            lax.rem(self.lon + (dlon + N_LON), N_LON),
        )

    def twin(self):
        return (self.y * 2 + (1 - self.core), self.lon)

    def index(self, axis):
        is_x = lax.div((2 - axis) * (1 - axis), 2)
        is_y = axis * (2 - axis)
        is_z = lax.div(axis * (axis - 1), 2)
        return self.x * is_x + self.y * is_y + self.z * is_z

    def shifted(self, axis, d):
        is_x = lax.div((2 - axis) * (1 - axis), 2)
        is_y = axis * (2 - axis)
        is_z = lax.div(axis * (axis - 1), 2)
        x = lax.rem(self.x + d * is_x, 4)
        y = lax.rem(self.y + d * is_y, 4)
        z = lax.rem(self.z + d * is_z, 4)
        return (y * 2 + self.core, x * 4 + z)

    def axis(self, b, level):
        return lax.rem(self.core + (b + level), 3)


class Reduce:
    def __init__(self, place, nb, gb, rc, s0, r1, s1, r2, s2, r3, fin, send, recv):
        self.p, self.nb = place, nb
        self.gb, self.rc, self.s0, self.r1, self.s1 = gb, rc, s0, r1, s1
        self.r2, self.s2, self.r3, self.fin = r2, s2, r3, fin
        self.send, self.recv = send, recv
        self.copies = {}

    def pack(self, j, val):
        for b in range(4):
            part = val[:, b * LANE : (b + 1) * LANE].astype(BF16)
            self.gb[:, b, :, :, j] = part.reshape(2, 4, 4, 16, LANE)

    def copy(self, step, k, src, dst, device):
        at = 1 + (step - 1) * 12 + k if 1 <= step <= 5 else (0 if step == 0 else 61)
        c = pltpu.make_async_remote_copy(
            src_ref=src,
            dst_ref=dst,
            send_sem=self.send.at[at],
            recv_sem=self.recv.at[at],
            device_id=device,
            device_id_type=MESH,
        )
        c.start()
        self.copies.setdefault(step, []).append(c)

    def wait(self, step):
        for c in self.copies[step]:
            c.wait_recv()

    def spread(self, step, level, src, dst):
        for b in range(4):
            axis = self.p.axis(b, level)
            for d in (2, 1, 3):
                there = lax.rem(self.p.index(axis) + d, 4)
                self.copy(
                    step, b * 3 + d - 1, src(b, there), dst(b, d), self.p.shifted(axis, d)
                )

    def step(self, k):
        h = self.p.core
        own = [self.p.index(self.p.axis(b, 0)) for b in range(4)]
        own2 = [self.p.index(self.p.axis(b, 1)) for b in range(4)]
        if k == 0:
            self.copy(0, 0, self.gb.at[1 - h], self.rc, self.p.twin())
        elif k == 1:
            self.wait(0)
            for b in range(4):
                mine = self.gb[h, b].astype(F32)
                self.s0[b] = (mine + self.rc[b].astype(F32)).astype(BF16)
            self.spread(1, 0, lambda b, i: self.s0.at[b, i], lambda b, d: self.r1.at[b, d - 1])
        elif k == 2:
            self.wait(1)
            for b in range(4):
                total = self.s0[b, own[b]].astype(F32)
                for d in range(3):
                    total += self.r1[b, d].astype(F32)
                self.s1[b] = total.astype(BF16)
            self.spread(2, 1, lambda b, i: self.s1.at[b, i], lambda b, d: self.r2.at[b, d - 1])
        elif k == 3:
            self.wait(2)
            for b in range(4):
                total = self.s1[b, own2[b]].astype(F32)
                for d in range(3):
                    total += self.r2[b, d].astype(F32)
                self.s2[b] = total.astype(BF16)
            self.spread(3, 2, lambda b, i: self.s2.at[b], lambda b, d: self.r3.at[b, d - 1])
        elif k == 4:
            self.wait(3)
            for b in range(4):
                near = self.s2[b].astype(F32) + self.r3[b, 1].astype(F32)
                far = self.r3[b, 0].astype(F32) + self.r3[b, 2].astype(F32)
                self.fin[h, b, own[b], own2[b]] = (near + far).astype(BF16)

            def piece(b, _):
                return self.fin.at[h, b, own[b], own2[b]]

            self.spread(4, 1, piece, piece)
        elif k == 5:
            self.wait(4)

            def piece(b, _):
                return self.fin.at[h, b, own[b]]

            self.spread(5, 0, piece, piece)
        elif k == 6:
            self.wait(5)
            self.copy(6, 0, self.fin.at[h], self.fin.at[h], self.p.twin())
        elif k == 7:
            self.wait(6)

    def drain(self):
        for group in self.copies.values():
            for c in group:
                c.wait_send()


class Vectors:
    def __init__(self, place, val, slots, send, recv):
        self.p, self.val, self.slots, self.send, self.recv = place, val, slots, send, recv
        self.copies = []

    def start(self, k):
        axis = k - 1
        hops = ((0, self.p.twin()),) if k == 0 else tuple(
            (d, self.p.shifted(jnp.int32(axis), d)) for d in (1, 2, 3)
        )
        for d, device in hops:
            at = 0 if k == 0 else 3 * (k - 1) + d
            c = pltpu.make_async_remote_copy(
                src_ref=self.val.at[k],
                dst_ref=self.slots.at[at],
                send_sem=self.send.at[at],
                recv_sem=self.recv.at[at],
                device_id=device,
                device_id_type=MESH,
            )
            c.start()
            self.copies.append((k, c))

    def finish(self, k):
        for j, c in self.copies:
            if j == k:
                c.wait_recv()
        if k == 0:
            self.val[1] = self.val[0] + self.slots[0]
        else:
            at = 3 * (k - 1)
            near = self.val[k] + self.slots[at + 2]
            far = self.slots[at + 1] + self.slots[at + 3]
            self.val[k + 1] = near + far

    def drain(self):
        for _, c in self.copies:
            c.wait_send()


def layer(
    nodes_h, edges_h, senders, receivers, live, send_rows, cot_h,
    wei_h, eib, weo_h, eob, egain, wni_h, nib, wno_h, nob, ngain,
    new_nodes_h, node_grad_h, edge_grad_h, fin_a_h, fin_b_h, fin_c_h, vec_h,
    nodes, edges, cot, wei, weo, wni, wno,
    ohs, oht, ohr, pre, hid, normed, scale, gath, prnd,
    table, grad_rows, zb, halo_out, halo_in, back_out, back_in, sendt,
    new_nodes, node_base, node_grad, summed, acc,
    bufs_a, bufs_b, bufs_c, vec, vec_slots,
    in_sem, out_sem, halo_send, halo_recv, sems_a, sems_b, sems_c, sems_v,
):
    place = Place()
    staging = normed
    prd = ohs.at[:, 0:D]

    def load(k, src, dst):
        c = pltpu.make_async_copy(src, dst, in_sem.at[k])
        c.start()
        return c

    def store(k, src, dst):
        c = pltpu.make_async_copy(src, dst, out_sem.at[k])
        c.start()
        return c

    c_nodes = load(0, nodes_h, nodes)
    c_wei = load(1, wei_h, wei)
    c_edges = load(2, edges_h, edges)
    c_weo = load(3, weo_h, weo)
    c_wni = load(4, wni_h, wni)
    c_wno = load(5, wno_h, wno)
    c_cot = load(6, cot_h, cot)

    barrier = pltpu.get_barrier_semaphore()
    partners = [place.neighbour(n) for n in range(8)] + [place.twin()]
    for axis in range(3):
        for d in (1, 2, 3):
            partners.append(place.shifted(jnp.int32(axis), d))
    for device in partners:
        pl.semaphore_signal(barrier, inc=1, device_id=device, device_id_type=MESH)

    red_a = Reduce(place, 3, *bufs_a, *sems_a)
    red_b = Reduce(place, 2, *bufs_b, *sems_b)
    red_c = Reduce(place, 2, *bufs_c, *sems_c)
    red_v = Vectors(place, vec, vec_slots, *sems_v)

    c_nodes.wait()
    picks = []
    for k in range(2):
        col = column_of(send_rows[:, k * LANE : (k + 1) * LANE])
        picks.append(jnp.concatenate([hot(col == lanes(j * LANE)) for j in range(4)], axis=1))
    listed = dot(jnp.concatenate(picks, axis=0), nodes[...]).astype(BF16)
    halo_out[...] = listed.reshape(8, SLOT, D)
    pl.semaphore_wait(barrier, len(partners))

    def exchange(src, dst, base):
        copies = []
        for n in range(8):
            c = pltpu.make_async_remote_copy(
                src_ref=src.at[n],
                dst_ref=dst.at[7 - n],
                send_sem=halo_send.at[base + n],
                recv_sem=halo_recv.at[base + 7 - n],
                device_id=place.neighbour(n),
                device_id_type=MESH,
            )
            c.start()
            copies.append(c)
        return copies

    halo = exchange(halo_out, halo_in, 0)

    rowi = lax.broadcasted_iota(I32, (NODE, LANE), 0)
    for k in range(2):
        row = send_rows[:, k * LANE : (k + 1) * LANE]
        sendt[:, k * LANE : (k + 1) * LANE] = hot(rowi == row)
    c_wei.wait()
    table[0:NODE, :] = dot(nodes[...], wei[D : 2 * D, :]).astype(BF16)
    table[TABLE:WIDE, :] = dot(nodes[...], wei[2 * D : 3 * D, :]).astype(BF16)
    c_edges.wait()

    def early(c, _):
        base = pl.multiple_of(c * CHUNK, CHUNK)
        rows = pl.ds(base, CHUNK)
        pre[rows, :] = dot(edges[rows, :], wei[0:D, :]) + eib[...]
        for j in range(CHUNK // LANE):
            s_row = senders[pl.ds(c * (CHUNK // LANE) + j, 1), :]
            r_row = receivers[pl.ds(c * (CHUNK // LANE) + j, 1), :]
            s_col, r_col = column_of(s_row), column_of(r_row)
            here = pl.ds(pl.multiple_of(base + j * LANE, LANE), LANE)
            for k in range(TABLE // LANE):
                ohs[here, k * LANE : (k + 1) * LANE] = hot(s_col == lanes(k * LANE))
            for k in range(NODE // LANE):
                ohr[here, k * LANE : (k + 1) * LANE] = hot(r_col == lanes(k * LANE))
            ids = lax.broadcasted_iota(I32, (TABLE, LANE), 0)
            oht[0:TABLE, here] = hot(ids == s_row)
            oht[TABLE:WIDE, here] = hot(rowi == r_row)
        return 0

    lax.fori_loop(0, STEPS, early, 0)

    for c in halo:
        c.wait_recv()
    incoming = halo_in[...].reshape(PEER, D)
    table[NODE:TABLE, :] = dot(incoming, wei[D : 2 * D, :]).astype(BF16)
    c_weo.wait()

    def is_live(base):
        return lax.broadcasted_iota(I32, (CHUNK, D), 0) < live[0] - base

    def forward(c, _):
        base = pl.multiple_of(c * CHUNK, CHUNK)
        rows = pl.ds(base, CHUNK)
        z = pre[rows, :] + dot(ohs[rows, :], table[0:TABLE, :])
        z = z + dot(ohr[rows, :], table[TABLE:WIDE, :])
        h, slope = silu_parts(z)
        hid[rows, :] = h.astype(BF16)
        pre[rows, :] = slope
        post = dot(hid[rows, :], weo[...]) + eob[...]
        unit, inv = normalize(post)
        normed[rows, :] = unit.astype(BF16)
        scale[rows, :] = inv
        new = edges[rows, :].astype(F32) + unit * egain[...]
        gath[rows, :] = jnp.where(is_live(base), new, 0.0).astype(BF16)
        return 0

    lax.fori_loop(0, STEPS, forward, 0)
    summed[...] = dot(oht[TABLE:WIDE, :], gath[...]).astype(BF16)

    c_wni.wait()
    c_wno.wait()
    c_cot.wait()
    z = dot(nodes[...], wni[0:D, :]) + dot(summed[...], wni[D : 2 * D, :]) + nib[...]
    h, slope = silu_parts(z)
    h = h.astype(BF16)
    unit, inv = normalize(dot(h, wno[...]) + nob[...])
    new_nodes[...] = (nodes[...].astype(F32) + unit * ngain[...]).astype(BF16)
    s_nodes = store(0, new_nodes, new_nodes_h)
    cotangent = cot[...].astype(F32)
    vec[0, 5:6, :] = col_sum(cotangent * unit)
    post_grad = norm_back(cotangent * ngain[...], unit, inv)
    vec[0, 4:5, :] = col_sum(post_grad)
    post_round = post_grad.astype(BF16)
    pre_grad = dot_rt(post_round, wno[...]) * slope
    vec[0, 3:4, :] = col_sum(pre_grad)
    pre_round = pre_grad.astype(BF16)
    grad_rows[...] = dot_rt(pre_round, wni[D : 2 * D, :]).astype(BF16)
    red_a.pack(2, dot_lt(h, post_round))
    red_a.pack(0, dot_lt(nodes[...], pre_round))
    red_a.pack(1, dot_lt(summed[...], pre_round))
    red_a.step(0)
    node_base[...] = cotangent + dot_rt(pre_round, wni[0:D, :])

    acc[...] = jnp.zeros_like(acc)

    def backward(c, _):
        base = pl.multiple_of(c * CHUNK, CHUNK)
        rows = pl.ds(base, CHUNK)
        g = jnp.where(is_live(base), dot(ohr[rows, :], grad_rows[...]), 0.0)
        gath[rows, :] = g.astype(BF16)
        unit = normed[rows, :].astype(F32)
        acc[2:3, :] += col_sum(g * unit)
        post_grad = norm_back(g * egain[...], unit, scale[rows, :])
        acc[1:2, :] += col_sum(post_grad)
        prnd[rows, :] = post_grad.astype(BF16)
        pre_grad = dot_rt(prnd[rows, :], weo[...]) * pre[rows, :]
        acc[0:1, :] += col_sum(pre_grad)
        prd[rows, :] = pre_grad.astype(BF16)
        return 0

    for c in range(STEPS):
        backward(c, 0)
        red_a.step(c + 1)
    vec[0, 0:3, :] = acc[0:3, :]
    vec[0, 6:8, :] = jnp.zeros((2, D), F32)
    red_v.start(0)

    red_b.pack(0, dot_lt(edges[...], prd[...]))
    red_b.pack(1, dot_lt(hid[...], prnd[...]))
    red_b.step(0)
    red_a.step(5)
    red_v.finish(0)
    red_v.start(1)
    for j in range(0, WIDE, 256):
        zb[j : j + 256, :] = dot(oht[j : j + 256, :], prd[...]).astype(BF16)
    red_b.step(1)
    red_c.pack(0, dot_lt(nodes[...], zb[0:NODE, :]) + dot_lt(incoming, zb[NODE:TABLE, :]))
    red_c.pack(1, dot_lt(nodes[...], zb[TABLE:WIDE, :]))
    red_c.step(0)
    red_a.step(6)
    red_v.finish(1)
    red_v.start(2)

    back = dot_rt(zb[NODE:TABLE, :], wei[D : 2 * D, :]).astype(BF16)
    back_out[...] = back.reshape(8, SLOT, D)
    returning = exchange(back_out, back_in, 8)
    red_b.step(2)
    node_base[...] += dot_rt(zb[0:NODE, :], wei[D : 2 * D, :])
    node_base[...] += dot_rt(zb[TABLE:WIDE, :], wei[2 * D : 3 * D, :])
    red_c.step(1)
    red_v.finish(2)
    red_v.start(3)

    stores = []

    def edge_out(c):
        rows = pl.ds(c * CHUNK, CHUNK)
        grad = dot_rt(prd[rows, :], wei[0:D, :])
        staging[rows, :] = (gath[rows, :].astype(F32) + grad).astype(BF16)
        stores.append(store(2 + c, staging.at[rows], edge_grad_h.at[rows]))

    edge_out(0)
    red_b.step(3)
    edge_out(1)
    red_c.step(2)
    red_b.step(4)
    edge_out(2)
    red_c.step(3)
    edge_out(3)
    red_b.step(5)
    for c in returning:
        c.wait_recv()
    owned = dot(sendt[...], back_in[...].reshape(PEER, D))
    node_grad[...] = (node_base[...] + owned).astype(BF16)
    stores.append(store(1, node_grad, node_grad_h))
    red_v.finish(3)
    stores.append(store(6, vec.at[4], vec_h))
    red_a.step(7)
    stores.append(store(7, red_a.fin, fin_a_h))
    red_c.step(4)
    red_b.step(6)
    red_c.step(5)
    red_b.step(7)
    stores.append(store(8, red_b.fin, fin_b_h))
    red_c.step(6)
    red_c.step(7)
    stores.append(store(9, red_c.fin, fin_c_h))
    for c in halo + returning:
        c.wait_send()
    for red in (red_a, red_b, red_c, red_v):
        red.drain()
    s_nodes.wait()
    for c in stores:
        c.wait()


def fin_shape(nb):
    return (2, 4, 4, 4, nb, 16, LANE)


def reduce_bufs(nb):
    tile = (nb, 16, LANE)
    return (
        pltpu.VMEM(fin_shape(nb), BF16),
        pltpu.VMEM((4, 4, 4) + tile, BF16),
        pltpu.VMEM((4, 4, 4) + tile, BF16),
        pltpu.VMEM((4, 3, 4) + tile, BF16),
        pltpu.VMEM((4, 4) + tile, BF16),
        pltpu.VMEM((4, 3) + tile, BF16),
        pltpu.VMEM((4,) + tile, BF16),
        pltpu.VMEM((4, 3) + tile, BF16),
        pltpu.VMEM(fin_shape(nb), BF16),
    )


def sem_pair(n):
    return (pltpu.SemaphoreType.DMA((n,)), pltpu.SemaphoreType.DMA((n,)))


def widen(fa, fb, fc, vec, edge_inner, edge_outer, node_inner, node_outer, *vecs):
    def put(src, j, out, k):
        for b in range(4):
            tile = src[0, b, 0, :, j].reshape(64, LANE).astype(F32)
            out[k, 0, :, b * LANE : (b + 1) * LANE] = tile

    put(fa, 0, node_inner, 0)
    put(fa, 1, node_inner, 1)
    put(fa, 2, node_outer, 0)
    put(fb, 0, edge_inner, 0)
    put(fb, 1, edge_outer, 0)
    put(fc, 0, edge_inner, 1)
    put(fc, 1, edge_inner, 2)
    for k in range(6):
        vecs[k][...] = vec[k : k + 1, :]


def unpack(fa, fb, fc, vec):
    def fin_spec(nb):
        return pl.BlockSpec((1, 4, 1, 4, nb, 16, LANE), lambda h, i: (h, 0, i, 0, 0, 0, 0))

    def out_spec(nb):
        return pl.BlockSpec((nb, 1, 64, D), lambda h, i: (0, h * 4 + i, 0, 0))

    counts = (3, 1, 2, 1)
    outs = pl.pallas_call(
        widen,
        grid=(2, 4),
        out_shape=[jax.ShapeDtypeStruct((n, 8, 64, D), F32) for n in counts]
        + [jax.ShapeDtypeStruct((1, D), F32)] * 6,
        in_specs=[fin_spec(3), fin_spec(2), fin_spec(2), pl.BlockSpec((8, D), lambda h, i: (0, 0))],
        out_specs=[out_spec(n) for n in counts]
        + [pl.BlockSpec((1, D), lambda h, i: (0, 0))] * 6,
        name="widen",
    )(fa, fb, fc, vec)
    mats = [o.reshape(n * D, D) for o, n in zip(outs, counts)]
    return mats, [v.reshape(D) for v in outs[4:]]


def body(
    node_states, edge_states, senders, receivers, live_count, send_rows, node_cotangent,
    edge_inner, edge_inbias, edge_outer, edge_outbias, edge_gain,
    node_inner, node_inbias, node_outer, node_outbias, node_gain,
):
    hbm = pl.BlockSpec(memory_space=pl.ANY)
    vm = pl.BlockSpec(memory_space=pltpu.VMEM)
    sm = pl.BlockSpec(memory_space=pltpu.SMEM)

    def row(v):
        return v.reshape(1, D)

    def v(shape, dtype=BF16):
        return pltpu.VMEM(shape, dtype)

    outs = pl.pallas_call(
        layer,
        out_shape=[
            jax.ShapeDtypeStruct((NODE, D), BF16),
            jax.ShapeDtypeStruct((NODE, D), BF16),
            jax.ShapeDtypeStruct((EDGE, D), BF16),
            jax.ShapeDtypeStruct(fin_shape(3), BF16),
            jax.ShapeDtypeStruct(fin_shape(2), BF16),
            jax.ShapeDtypeStruct(fin_shape(2), BF16),
            jax.ShapeDtypeStruct((8, D), F32),
        ],
        in_specs=[
            hbm, hbm, vm, vm, sm, vm, hbm,
            hbm, vm, hbm, vm, vm, hbm, vm, hbm, vm, vm,
        ],
        out_specs=[hbm] * 7,
        scratch_shapes=[
            v((NODE, D)), v((EDGE, D)), v((NODE, D)),
            v((3 * D, D)), v((D, D)), v((2 * D, D)), v((D, D)),
            v((EDGE, TABLE)), v((WIDE, EDGE)), v((EDGE, NODE)),
            v((EDGE, D), F32), v((EDGE, D)), v((EDGE, D)), v((EDGE, 1), F32),
            v((EDGE, D)), v((EDGE, D)),
            v((WIDE, D)), v((NODE, D)), v((WIDE, D)),
            v((8, SLOT, D)), v((8, SLOT, D)), v((8, SLOT, D)), v((8, SLOT, D)),
            v((NODE, PEER)),
            v((NODE, D)), v((NODE, D), F32), v((NODE, D)), v((NODE, D)), v((8, D), F32),
            reduce_bufs(3), reduce_bufs(2), reduce_bufs(2),
            v((5, 8, D), F32), v((10, 8, D), F32),
            pltpu.SemaphoreType.DMA((7,)), pltpu.SemaphoreType.DMA((10,)),
            pltpu.SemaphoreType.DMA((16,)), pltpu.SemaphoreType.DMA((16,)),
            sem_pair(62), sem_pair(62), sem_pair(62), sem_pair(10),
        ],
        compiler_params=pltpu.CompilerParams(
            collective_id=0, has_side_effects=True, vmem_limit_bytes=63 * 2**20
        ),
        name="layer",
    )(
        node_states, edge_states, senders.reshape(16, LANE), receivers.reshape(16, LANE),
        live_count, send_rows, node_cotangent,
        edge_inner, row(edge_inbias), edge_outer, row(edge_outbias), row(edge_gain),
        node_inner, row(node_inbias), node_outer, row(node_outbias), row(node_gain),
    )
    new_nodes, node_grad, edge_grad, fa, fb, fc, vec = outs
    mats, vecs = unpack(fa, fb, fc, vec)
    return (
        new_nodes, node_grad, edge_grad,
        mats[0], vecs[0], mats[1], vecs[1], vecs[2],
        mats[2], vecs[3], mats[3], vecs[4], vecs[5],
    )


def solution(mesh):
    nodes = P(("lat", "lon"), None)
    flat = P(("lat", "lon"))
    return jax.shard_map(
        body,
        mesh=mesh,
        in_specs=(nodes, nodes, flat, flat, flat, nodes, nodes) + (P(),) * 10,
        out_specs=(nodes, nodes, nodes) + (P(),) * 10,
        check_vma=False,
    )
```

profile of v0, /device:TPU:1, one launch (start us, length us, event | category | flops | bytes accessed | tf_op | source)
XLA Modules:
  0.0 95.4 jit_solution(14991834867547338918)
XLA Ops:
  1.3 83.5 %layer.1 = (bf16[512,512]{1,0:T(8,128)(2,1)}, bf16[512,512]{1,0:T(8,128)(2,1)}, bf16[2048,512]{1,0:T(8,128)(2,1)}, bf16[2,4,4,4,3,16,128]{6,5,4,3,2,1,0:T(8,128)...) custom-call(bf16[512,512]{1,0:T(8,128)(2,1)} %nodes_h.1, ...), custom_call_target="tpu_custom_call" | custom-call | tf_op jit(solution)/shard_map/layer/pallas_call | solution.py:577
  84.8 0.0 copy-start.2
  84.8 0.0 copy-start.1
  84.8 0.0 copy-start
  84.8 7.6 %widen.1 = (f32[3,8,64,512]{3,2,1,0:T(8,128)}, f32[1,8,64,512]{3,2,1,0:T(8,128)}, f32[2,8,64,512]{3,2,1,0:T(8,128)}, f32[1,8,64,512]{3,2,1,0:T(8,128)}, f32[1,51...) custom-call(bf16[2,4,4,4,3,16,128]{6,5,4,3,2,1,0:T(8,128)(2,1)} %get, ...), custom_call_target="tpu_custom_call" | custom-call | tf_op jit(solution)/shard_map/widen/pallas_call | solution.py:548
  92.4 0.0 copy-done.2
  92.5 0.8 copy.34
  93.3 0.0 copy-done.1
  93.3 0.8 copy.35
  94.0 0.0 copy-done
  94.1 1.3 %copy.36 = bf16[2048,512]{1,0:T(8,128)(2,1)} copy(bf16[2048,512]{1,0:T(8,128)(2,1)S(1)} %copy-done) | data formatting | bytes 4194304
Async XLA Ops:
  84.8 7.7 %copy-start.2 = (bf16[512,512]{1,0:T(8,128)(2,1)S(1)}, bf16[512,512]{1,0:T(8,128)(2,1)}, u32[]{:S(2)}) copy-start(bf16[512,512]{1,0:T(8,128)(2,1)} %get-tuple-element.60) | copy-start | bytes 1572868
  84.8 8.5 %copy-start.1 = (bf16[512,512]{1,0:T(8,128)(2,1)S(1)}, bf16[512,512]{1,0:T(8,128)(2,1)}, u32[]{:S(2)}) copy-start(bf16[512,512]{1,0:T(8,128)(2,1)} %get-tuple-element.61) | copy-start | bytes 1572868
  84.8 9.3 %copy-start = (bf16[2048,512]{1,0:T(8,128)(2,1)S(1)}, bf16[2048,512]{1,0:T(8,128)(2,1)}, u32[]{:S(2)}) copy-start(bf16[2048,512]{1,0:T(8,128)(2,1)} %get-tuple-element.62) | copy-start | bytes 6291460
where the time goes:
time: 95.7 us; the launch traced here: 95.4 us
  Pallas kernels  91.1 us (95%)
  local copies, waits for them, and re-layouts  2.92 us (3%)
  between operations  1.35 us (1%)
    pallas_call x1, Pallas kernels, body(): pl.pallas_call(layer, out_shape=[jax.ShapeDtypeStruct((NODE, D), BF16), j...  83.5 us
    pallas_call x1, Pallas kernels, unpack(): pl.pallas_call(widen, grid=(2, 4), out_shape=[jax.ShapeDtypeStruct((n, 8,...  7.64 us
    unnamed x9, local copies, waits for them, and re-layouts  2.92 us

commit v1 on v0

v1 whole, which is shorter than its diff:
```python
import functools

import jax
import jax.numpy as jnp
from jax import lax
from jax.experimental import pallas as pl
from jax.experimental.pallas import tpu as pltpu
from jax.sharding import PartitionSpec as P

MESH = pl.DeviceIdType.MESH
F32 = jnp.float32
BF16 = jnp.bfloat16
I32 = jnp.int32
epsilon = 1e-05

D = 512
NODE = 512
EDGE = 2048
SLOT = 32
PEER = 256
TABLE = NODE + PEER
WIDE = TABLE + NODE
CHUNK = 512
STEPS = EDGE // CHUNK
PART = 256
PARTS = EDGE // PART
SUB = 32
SUBS = PART // SUB
LANE = 128
N_LAT = 8
N_LON = 16
OFFSETS = ((-1, -1), (-1, 0), (-1, 1), (0, -1), (0, 1), (1, -1), (1, 0), (1, 1))


def dot(a, b):
    return jnp.dot(a, b, preferred_element_type=F32)


def dot_rt(a, b):
    return lax.dot_general(a, b, (((1,), (1,)), ((), ())), preferred_element_type=F32)


def dot_lt(a, b):
    return lax.dot_general(a, b, (((0,), (0,)), ((), ())), preferred_element_type=F32)


def row_mean(x):
    return jnp.sum(x, axis=-1, keepdims=True) * (1.0 / D)


def col_sum(x):
    return jnp.sum(x, axis=0, keepdims=True)


def silu_parts(z):
    sig = 0.5 + 0.5 * jnp.tanh(0.5 * z)
    h = z * sig
    return h, sig + h * (1.0 - sig)


def normalize(post):
    centered = post - row_mean(post)
    scale = lax.rsqrt(row_mean(centered * centered) + epsilon)
    return centered * scale, scale


def norm_back(t, normed, scale):
    return scale * (t - row_mean(t) - normed * row_mean(t * normed))


def column_of(row):
    return jnp.transpose(jnp.broadcast_to(row.astype(F32), (LANE, LANE))).astype(I32)


def lanes(base):
    return lax.broadcasted_iota(I32, (LANE, LANE), 1) + base


def hot(mask):
    return jnp.where(mask, 1.0, 0.0).astype(BF16)


class Place:
    def __init__(self):
        self.lat = lax.axis_index("lat")
        self.lon = lax.axis_index("lon")
        self.core = lax.rem(self.lat, 2)
        self.y = lax.div(self.lat, 2)
        self.x = lax.div(self.lon, 4)
        self.z = lax.rem(self.lon, 4)

    def neighbour(self, n):
        dlat, dlon = OFFSETS[n]
        return (
            lax.rem(self.lat + (dlat + N_LAT), N_LAT),
            lax.rem(self.lon + (dlon + N_LON), N_LON),
        )

    def twin(self):
        return (self.y * 2 + (1 - self.core), self.lon)

    def index(self, axis):
        is_x = lax.div((2 - axis) * (1 - axis), 2)
        is_y = axis * (2 - axis)
        is_z = lax.div(axis * (axis - 1), 2)
        return self.x * is_x + self.y * is_y + self.z * is_z

    def shifted(self, axis, d):
        is_x = lax.div((2 - axis) * (1 - axis), 2)
        is_y = axis * (2 - axis)
        is_z = lax.div(axis * (axis - 1), 2)
        x = lax.rem(self.x + d * is_x, 4)
        y = lax.rem(self.y + d * is_y, 4)
        z = lax.rem(self.z + d * is_z, 4)
        return (y * 2 + self.core, x * 4 + z)

    def axis(self, b, level):
        return lax.rem(self.core + (b + level), 3)


class Reduce:
    def __init__(self, place, streams, gb, rc, s0, r1, s1, r2, s2, r3, fin, send, recv):
        self.p, self.streams = place, streams
        self.gb, self.rc, self.s0, self.r1, self.s1 = gb, rc, s0, r1, s1
        self.r2, self.s2, self.r3, self.fin = r2, s2, r3, fin
        self.send, self.recv = send, recv
        self.copies = {}

    def pack(self, j, val):
        width = val.shape[1]
        self.gb[:, j] = val.astype(BF16).reshape(2, 4, 4, 16, width)

    def copy(self, step, k, src, dst, device):
        at = 1 + (step - 1) * 9 + k if 1 <= step <= 5 else (0 if step == 0 else 46)
        c = pltpu.make_async_remote_copy(
            src_ref=src,
            dst_ref=dst,
            send_sem=self.send.at[at],
            recv_sem=self.recv.at[at],
            device_id=device,
            device_id_type=MESH,
        )
        c.start()
        self.copies.setdefault(step, []).append(c)

    def wait(self, step):
        for c in self.copies[step]:
            c.wait_recv()

    def spread(self, step, level, src, dst):
        for n, part in enumerate(self.streams):
            axis = self.p.axis(n, level)
            for d in (2, 1, 3):
                there = lax.rem(self.p.index(axis) + d, 4)
                self.copy(
                    step, n * 3 + d - 1, src(n, part, there), dst(n, part, d), self.p.shifted(axis, d)
                )

    def step(self, k):
        h = self.p.core
        count = len(self.streams)
        own = [self.p.index(self.p.axis(n, 0)) for n in range(count)]
        own2 = [self.p.index(self.p.axis(n, 1)) for n in range(count)]
        if k == 0:
            self.copy(0, 0, self.gb.at[1 - h], self.rc, self.p.twin())
        elif k == 1:
            self.wait(0)
            for part in self.streams:
                mine = self.gb[h, part].astype(F32)
                self.s0[part] = (mine + self.rc[part].astype(F32)).astype(BF16)
            self.spread(
                1, 0, lambda n, part, i: self.s0.at[part, i], lambda n, part, d: self.r1.at[d - 1, part]
            )
        elif k == 2:
            self.wait(1)
            for n, part in enumerate(self.streams):
                total = self.s0[part, own[n]].astype(F32)
                for d in range(3):
                    total += self.r1[d, part].astype(F32)
                self.s1[part] = total.astype(BF16)
            self.spread(
                2, 1, lambda n, part, i: self.s1.at[part, i], lambda n, part, d: self.r2.at[d - 1, part]
            )
        elif k == 3:
            self.wait(2)
            for n, part in enumerate(self.streams):
                total = self.s1[part, own2[n]].astype(F32)
                for d in range(3):
                    total += self.r2[d, part].astype(F32)
                self.s2[part] = total.astype(BF16)
            self.spread(
                3, 2, lambda n, part, i: self.s2.at[part], lambda n, part, d: self.r3.at[d - 1, part]
            )
        elif k == 4:
            self.wait(3)
            for n, part in enumerate(self.streams):
                near = self.s2[part].astype(F32) + self.r3[1, part].astype(F32)
                far = self.r3[0, part].astype(F32) + self.r3[2, part].astype(F32)
                self.fin[h, part, own[n], own2[n]] = (near + far).astype(BF16)

            def piece(n, part, _):
                return self.fin.at[h, part, own[n], own2[n]]

            self.spread(4, 1, piece, piece)
        elif k == 5:
            self.wait(4)

            def piece(n, part, _):
                return self.fin.at[h, part, own[n]]

            self.spread(5, 0, piece, piece)
        elif k == 6:
            self.wait(5)
            self.copy(6, 0, self.fin.at[h], self.fin.at[h], self.p.twin())
        elif k == 7:
            self.wait(6)

    def drain(self):
        for group in self.copies.values():
            for c in group:
                c.wait_send()


class Vectors:
    def __init__(self, place, val, slots, send, recv):
        self.p, self.val, self.slots, self.send, self.recv = place, val, slots, send, recv
        self.copies = []

    def start(self, k):
        axis = k - 1
        hops = ((0, self.p.twin()),) if k == 0 else tuple(
            (d, self.p.shifted(jnp.int32(axis), d)) for d in (1, 2, 3)
        )
        for d, device in hops:
            at = 0 if k == 0 else 3 * (k - 1) + d
            c = pltpu.make_async_remote_copy(
                src_ref=self.val.at[k],
                dst_ref=self.slots.at[at],
                send_sem=self.send.at[at],
                recv_sem=self.recv.at[at],
                device_id=device,
                device_id_type=MESH,
            )
            c.start()
            self.copies.append((k, c))

    def finish(self, k):
        for j, c in self.copies:
            if j == k:
                c.wait_recv()
        if k == 0:
            self.val[1] = self.val[0] + self.slots[0]
        else:
            at = 3 * (k - 1)
            near = self.val[k] + self.slots[at + 2]
            far = self.slots[at + 1] + self.slots[at + 3]
            self.val[k + 1] = near + far

    def drain(self):
        for _, c in self.copies:
            c.wait_send()


def layer(
    nodes_h, edges_h, senders, receivers, live, send_rows, cot_h,
    wei_h, eib, weo_h, eob, egain, wni_h, nib, wno_h, nob, ngain,
    new_nodes_h, node_grad_h, edge_grad_h, fin_a_h, fin_o_h, fin_b_h, fin_c_h, vec_h,
    nodes, edges, cot, wei, weo, wni, wno,
    ohs, oht, ohr, edges_t, pre, hid, normed, scale, prnd, staging, post,
    table, grad_rows, zb, halo_out, halo_in, back_out, back_in, sendt,
    new_nodes, node_base, node_grad, summed, sum_acc, outer_acc,
    npre, npost, nhid, npost_round, npre_round, acc,
    bufs_a, bufs_o, bufs_b, bufs_c, vec, vec_slots,
    in_sem, out_sem, halo_send, halo_recv, sems_a, sems_o, sems_b, sems_c, sems_v,
):
    place = Place()
    prd = ohs

    def load(k, src, dst):
        c = pltpu.make_async_copy(src, dst, in_sem.at[k])
        c.start()
        return c

    def store(k, src, dst):
        c = pltpu.make_async_copy(src, dst, out_sem.at[k])
        c.start()
        return c

    c_nodes = load(0, nodes_h, nodes)
    c_wei = load(1, wei_h, wei)
    c_edges = load(2, edges_h, edges)
    c_wni = load(4, wni_h, wni)
    c_weo = load(3, weo_h, weo)
    c_wno = load(5, wno_h, wno)
    c_cot = load(6, cot_h, cot)

    barrier = pltpu.get_barrier_semaphore()
    partners = [place.neighbour(n) for n in range(8)] + [place.twin()]
    for axis in range(3):
        for d in (1, 2, 3):
            partners.append(place.shifted(jnp.int32(axis), d))
    for device in partners:
        pl.semaphore_signal(barrier, inc=1, device_id=device, device_id_type=MESH)

    thirds = (slice(0, 1), slice(1, 2), slice(2, 3))
    red_a = Reduce(place, thirds, *bufs_a, *sems_a)
    red_o = Reduce(place, (slice(0, 2), slice(2, 3), slice(3, 4)), *bufs_o, *sems_o)
    red_b = Reduce(place, thirds, *bufs_b, *sems_b)
    red_c = Reduce(place, thirds, *bufs_c, *sems_c)
    red_v = Vectors(place, vec, vec_slots, *sems_v)

    picks = []
    for k in range(2):
        col = column_of(send_rows[:, k * LANE : (k + 1) * LANE])
        picks.append(jnp.concatenate([hot(col == lanes(j * LANE)) for j in range(4)], axis=1))
    picks = jnp.concatenate(picks, axis=0)
    c_nodes.wait()
    halo_out[...] = dot(picks, nodes[...]).astype(BF16).reshape(8, SLOT, D)
    pl.semaphore_wait(barrier, len(partners))

    def exchange(src, dst, base):
        copies = []
        for n in range(8):
            c = pltpu.make_async_remote_copy(
                src_ref=src.at[n],
                dst_ref=dst.at[7 - n],
                send_sem=halo_send.at[base + n],
                recv_sem=halo_recv.at[base + 7 - n],
                device_id=place.neighbour(n),
                device_id_type=MESH,
            )
            c.start()
            copies.append(c)
        return copies

    halo = exchange(halo_out, halo_in, 0)

    rowi = lax.broadcasted_iota(I32, (NODE, LANE), 0)
    for k in range(2):
        row = send_rows[:, k * LANE : (k + 1) * LANE]
        sendt[:, k * LANE : (k + 1) * LANE] = hot(rowi == row)
    acc[...] = jnp.zeros_like(acc)
    c_wei.wait()
    table[0:NODE, :] = dot(nodes[...], wei[D : 2 * D, :]).astype(BF16)
    table[TABLE:WIDE, :] = dot(nodes[...], wei[2 * D : 3 * D, :]).astype(BF16)
    c_edges.wait()

    def early(c, _):
        base = pl.multiple_of(c * CHUNK, CHUNK)
        rows = pl.ds(base, CHUNK)
        pre[rows, :] = dot(edges[rows, :], wei[0:D, :]) + eib[...]
        edges_t[:, rows] = jnp.transpose(edges[rows, :])
        for j in range(CHUNK // LANE):
            s_row = senders[pl.ds(c * (CHUNK // LANE) + j, 1), :]
            r_row = receivers[pl.ds(c * (CHUNK // LANE) + j, 1), :]
            s_col, r_col = column_of(s_row), column_of(r_row)
            here = pl.ds(pl.multiple_of(base + j * LANE, LANE), LANE)
            for k in range(TABLE // LANE):
                ohs[here, k * LANE : (k + 1) * LANE] = hot(s_col == lanes(k * LANE))
            for k in range(NODE // LANE):
                ohr[here, k * LANE : (k + 1) * LANE] = hot(r_col == lanes(k * LANE))
            ids = lax.broadcasted_iota(I32, (TABLE, LANE), 0)
            oht[0:TABLE, here] = hot(ids == s_row)
            oht[TABLE:WIDE, here] = hot(rowi == r_row)
        return 0

    lax.fori_loop(0, STEPS, early, 0)
    c_wni.wait()
    npre[...] = dot(nodes[...], wni[0:D, :]) + nib[...]
    c_weo.wait()
    c_wno.wait()
    c_cot.wait()

    for c in halo:
        c.wait_recv()
    table[NODE:TABLE, :] = dot(halo_in[...].reshape(PEER, D), wei[D : 2 * D, :]).astype(BF16)

    def part(t, s):
        return slice(t * PART + s * SUB, t * PART + (s + 1) * SUB)

    def whole(t):
        return slice(t * PART, (t + 1) * PART)

    def live_rows(t, s):
        ids = lax.broadcasted_iota(I32, (SUB, LANE), 0)
        one = jnp.where(ids < live[0] - (t * PART + s * SUB), 1.0, 0.0)
        return jnp.concatenate([one] * (D // LANE), axis=1)

    def fwd_gather(t):
        rows = whole(t)
        z = dot(ohs[rows, :], table[0:TABLE, :]) + dot(ohr[rows, :], table[TABLE:WIDE, :])
        pre[rows, :] += z

    def fwd_silu(t):
        for s in range(SUBS):
            rows = part(t, s)
            h, slope = silu_parts(pre[rows, :])
            hid[rows, :] = h.astype(BF16)
            pre[rows, :] = slope

    def fwd_outer(t):
        post[t % 3] = dot(hid[whole(t), :], weo[...])

    def fwd_norm(t):
        for s in range(SUBS):
            rows = part(t, s)
            unit, inv = normalize(post[t % 3, s * SUB : (s + 1) * SUB, :] + eob[...])
            normed[rows, :] = unit.astype(BF16)
            scale[rows, :] = inv
            new = edges[rows, :].astype(F32) + unit * egain[...]
            prnd[rows, :] = (new * live_rows(t, s)).astype(BF16)

    def fwd_sum(t):
        got = dot(oht[TABLE:WIDE, whole(t)], prnd[whole(t), :])
        if t == 0:
            sum_acc[...] = got
        else:
            sum_acc[...] += got

    def at(f, t):
        if 0 <= t < PARTS:
            f(t)

    for t in range(PARTS + 3):
        at(fwd_gather, t)
        at(fwd_silu, t - 1)
        at(fwd_norm, t - 2)
        at(fwd_outer, t - 1)
        at(fwd_sum, t - 3)
    summed[...] = sum_acc[...].astype(BF16)

    def fold(x):
        return jnp.sum(x.reshape(x.shape[0] // 8, 8, x.shape[1]), axis=0)

    halves = (0, 1)
    for t in halves:
        npre[whole(t), :] += dot(summed[whole(t), :], wni[D : 2 * D, :])
    for t in halves:
        for s in range(SUBS):
            rows = part(t, s)
            h, slope = silu_parts(npre[rows, :])
            nhid[rows, :] = h.astype(BF16)
            npre[rows, :] = slope
        npost[whole(t), :] = dot(nhid[whole(t), :], wno[...])
    for t in halves:
        for s in range(SUBS):
            rows = part(t, s)
            unit, inv = normalize(npost[rows, :] + nob[...])
            new_nodes[rows, :] = (nodes[rows, :].astype(F32) + unit * ngain[...]).astype(BF16)
            cotangent = cot[rows, :].astype(F32)
            acc[5] += fold(cotangent * unit)
            grad = norm_back(cotangent * ngain[...], unit, inv)
            acc[4] += fold(grad)
            npost_round[rows, :] = grad.astype(BF16)
        grad = dot_rt(npost_round[whole(t), :], wno[...]) * npre[whole(t), :]
        acc[3] += fold(grad)
        npre_round[whole(t), :] = grad.astype(BF16)
    for t in halves:
        grad_rows[whole(t), :] = dot_rt(npre_round[whole(t), :], wni[D : 2 * D, :]).astype(BF16)
    s_nodes = store(0, new_nodes, new_nodes_h)

    def bwd_gather(t):
        post[t % 3] = dot(ohr[whole(t), :], grad_rows[...])

    def bwd_norm(t):
        for s in range(SUBS):
            rows = part(t, s)
            g = post[t % 3, s * SUB : (s + 1) * SUB, :] * live_rows(t, s)
            unit = normed[rows, :].astype(F32)
            acc[2] += fold(g * unit)
            grad = norm_back(g * egain[...], unit, scale[rows, :])
            acc[1] += fold(grad)
            prnd[rows, :] = grad.astype(BF16)

    def bwd_outer(t):
        rows = slice((t - 1) * PART, (t + 1) * PART)
        got = dot_lt(hid[rows, :], prnd[rows, :])
        if t == 1:
            outer_acc[...] = got
        else:
            outer_acc[...] += got

    for t in range(PARTS + 1):
        at(bwd_gather, t)
        at(bwd_norm, t - 1)
        if t == 1:
            red_a.pack(2, dot_lt(nhid[...], npost_round[...]))
        if t == 2:
            red_a.pack(0, dot_lt(nodes[...], npre_round[...]))
        if t == 3:
            red_a.pack(1, dot_lt(summed[...], npre_round[...]))
            red_a.step(0)
        if t == 4:
            node_base[...] = cot[...].astype(F32) + dot_rt(npre_round[...], wni[0:D, :])
        if t >= 4 and t % 2 == 0:
            bwd_outer(t - 3)
    red_a.step(1)
    bwd_outer(PARTS - 1)
    for j in range(4):
        red_o.pack(j, outer_acc[:, j * LANE : (j + 1) * LANE])
    red_o.step(0)

    def bwd_inner(t, cols):
        grad = dot_rt(prnd[whole(t), :], weo[cols, :]) * pre[whole(t), cols]
        acc[0, :, cols] += fold(grad)
        prd[whole(t), cols] = grad.astype(BF16)

    left, right = slice(0, D // 2), slice(D // 2, D)
    for t in range(PARTS):
        bwd_inner(t, left)

    def z_rows(j, cols):
        zb[j * PART : (j + 1) * PART, cols] = dot(
            oht[j * PART : (j + 1) * PART, :], prd[:, cols]
        ).astype(BF16)

    def inner_sums(red, cols):
        incoming = halo_in[...].reshape(PEER, D)
        red.pack(1, dot_lt(nodes[...], zb[0:NODE, cols]) + dot_lt(incoming, zb[NODE:TABLE, cols]))
        red.pack(2, dot_lt(nodes[...], zb[TABLE:WIDE, cols]))
        red.step(0)

    for j in range(WIDE // PART):
        z_rows(j, left)
        bwd_inner(j, right)
    for t in range(WIDE // PART, PARTS):
        bwd_inner(t, right)
    red_b.pack(0, dot(edges_t[...], prd[:, left]))
    inner_sums(red_b, left)
    red_a.step(2)
    red_o.step(1)
    vec[0, 0:6, :] = jnp.sum(acc[...], axis=1)
    vec[0, 6:8, :] = jnp.zeros((2, D), F32)
    red_v.start(0)
    for j in range(WIDE // PART):
        z_rows(j, right)
    red_b.step(1)
    red_c.pack(0, dot(edges_t[...], prd[:, right]))
    inner_sums(red_c, right)
    red_a.step(3)
    red_o.step(2)
    red_v.finish(0)
    red_v.start(1)

    back = dot_rt(zb[NODE:TABLE, :], wei[D : 2 * D, :]).astype(BF16)
    back_out[...] = back.reshape(8, SLOT, D)
    returning = exchange(back_out, back_in, 8)
    red_a.step(4)
    red_c.step(1)
    red_o.step(3)
    red_b.step(2)
    stores = []

    def edge_out(c):
        rows = pl.ds(c * CHUNK, CHUNK)
        grad = dot_rt(prd[rows, 0:D], wei[0:D, :]) + dot(ohr[rows, :], grad_rows[...])
        alive = lax.broadcasted_iota(I32, (CHUNK, D), 0) < live[0] - c * CHUNK
        staging[rows, :] = jnp.where(alive, grad, 0.0).astype(BF16)
        stores.append(store(2 + c, staging.at[rows], edge_grad_h.at[rows]))

    edge_out(0)
    red_v.finish(1)
    red_v.start(2)
    red_a.step(5)
    red_b.step(3)
    red_o.step(4)
    red_c.step(2)
    edge_out(1)
    red_b.step(4)
    red_o.step(5)
    red_c.step(3)
    edge_out(2)
    red_v.finish(2)
    red_v.start(3)
    red_b.step(5)
    red_c.step(4)
    red_o.step(6)
    edge_out(3)
    red_a.step(6)
    red_c.step(5)
    node_base[...] += dot_rt(zb[0:NODE, :], wei[D : 2 * D, :])
    node_base[...] += dot_rt(zb[TABLE:WIDE, :], wei[2 * D : 3 * D, :])
    for c in returning:
        c.wait_recv()
    owned = dot(sendt[...], back_in[...].reshape(PEER, D))
    node_grad[...] = (node_base[...] + owned).astype(BF16)
    stores.append(store(1, node_grad, node_grad_h))
    red_v.finish(3)
    stores.append(store(6, vec.at[4], vec_h))
    red_b.step(6)
    red_o.step(7)
    stores.append(store(8, red_o.fin, fin_o_h))
    red_a.step(7)
    stores.append(store(7, red_a.fin, fin_a_h))
    red_c.step(6)
    red_b.step(7)
    stores.append(store(9, red_b.fin, fin_b_h))
    red_c.step(7)
    stores.append(store(10, red_c.fin, fin_c_h))
    for c in halo + returning:
        c.wait_send()
    for red in (red_a, red_o, red_b, red_c, red_v):
        red.drain()
    s_nodes.wait()
    for c in stores:
        c.wait()


def fin_shape(nb, width):
    return (2, nb, 4, 4, 16, width)


FINS = ((3, D), (4, LANE), (3, D // 2), (3, D // 2))


def reduce_bufs(nb, width):
    tile = (16, width)
    return (
        pltpu.VMEM(fin_shape(nb, width), BF16),
        pltpu.VMEM((nb, 4, 4) + tile, BF16),
        pltpu.VMEM((nb, 4, 4) + tile, BF16),
        pltpu.VMEM((3, nb, 4) + tile, BF16),
        pltpu.VMEM((nb, 4) + tile, BF16),
        pltpu.VMEM((3, nb) + tile, BF16),
        pltpu.VMEM((nb,) + tile, BF16),
        pltpu.VMEM((3, nb) + tile, BF16),
        pltpu.VMEM(fin_shape(nb, width), BF16),
    )


def sem_pair(n):
    return (pltpu.SemaphoreType.DMA((n,)), pltpu.SemaphoreType.DMA((n,)))


def widen(
    fa, fo, fb, fc, vec, new_nodes, node_grad, edge_grad,
    new_nodes_o, node_grad_o, edge_grad_o, edge_inner, edge_outer, node_inner, node_outer,
    v0, v1, v2, v3, v4, v5,
    va, vo, vb, vc, vn, vg, ve, wide, in_sem, out_sem,
):
    outs = []

    def load(k, src, dst):
        c = pltpu.make_async_copy(src, dst, in_sem.at[k])
        c.start()
        return c

    def store(k, src, dst):
        c = pltpu.make_async_copy(src, dst, out_sem.at[k])
        c.start()
        outs.append(c)

    c_a = [load(h, fa.at[h], va.at[h]) for h in range(2)]
    c_b = [load(2 + h, fb.at[h], vb.at[h]) for h in range(2)]
    c_c = [load(4 + h, fc.at[h], vc.at[h]) for h in range(2)]
    c_o = load(6, fo, vo)
    c_e = [load(7 + k, edge_grad.at[pl.ds(k * 512, 512)], ve.at[pl.ds(k * 512, 512)]) for k in range(4)]
    c_n = load(11, new_nodes, vn)
    c_g = load(12, node_grad, vg)
    k_out = 0
    HALF = NODE // 2

    places = ((node_inner, 0), (node_inner, 512), (node_outer, 0))
    for h in range(2):
        c_a[h].wait()
        for j, (out, first) in enumerate(places):
            rows = pl.ds(j * 512 + h * HALF, HALF)
            wide[rows, :] = va[h, j].reshape(HALF, D).astype(F32)
            store(k_out, wide.at[rows], out.at[pl.ds(first + h * HALF, HALF)])
            k_out += 1
    for h in range(2):
        c_b[h].wait()
        c_c[h].wait()
        for j in range(3):
            rows = pl.ds(1536 + j * 512 + h * HALF, HALF)
            wide[rows, 0:HALF] = vb[h, j].reshape(HALF, HALF).astype(F32)
            wide[rows, HALF:D] = vc[h, j].reshape(HALF, HALF).astype(F32)
            store(k_out, wide.at[rows], edge_inner.at[pl.ds(j * 512 + h * HALF, HALF)])
            k_out += 1
    c_o.wait()
    for h in range(2):
        rows = pl.ds(3072 + h * HALF, HALF)
        for j in range(4):
            wide[rows, j * LANE : (j + 1) * LANE] = vo[h, j].reshape(HALF, LANE).astype(F32)
        store(k_out, wide.at[rows], edge_outer.at[pl.ds(h * HALF, HALF)])
        k_out += 1
    for k in range(4):
        c_e[k].wait()
        store(k_out, ve.at[pl.ds(k * 512, 512)], edge_grad_o.at[pl.ds(k * 512, 512)])
        k_out += 1
    c_n.wait()
    store(k_out, vn, new_nodes_o)
    c_g.wait()
    store(k_out + 1, vg, node_grad_o)
    for k, out in enumerate((v0, v1, v2, v3, v4, v5)):
        out[...] = vec[k : k + 1, :]
    for c in outs:
        c.wait()


def unpack(outs):
    new_nodes, node_grad, edge_grad, fa, fo, fb, fc, vec = outs
    hbm = pl.BlockSpec(memory_space=pl.ANY)
    vm = pl.BlockSpec(memory_space=pltpu.VMEM)
    shapes = [
        ((NODE, D), BF16), ((NODE, D), BF16), ((EDGE, D), BF16),
        ((3 * D, D), F32), ((D, D), F32), ((2 * D, D), F32), ((D, D), F32),
    ] + [((1, D), F32)] * 6
    scratch = [pltpu.VMEM(fin_shape(*f), BF16) for f in FINS]
    return pl.pallas_call(
        widen,
        out_shape=[jax.ShapeDtypeStruct(s, t) for s, t in shapes],
        in_specs=[hbm] * 4 + [vm] + [hbm] * 3,
        out_specs=[hbm] * 7 + [vm] * 6,
        scratch_shapes=scratch + [
            pltpu.VMEM((NODE, D), BF16), pltpu.VMEM((NODE, D), BF16), pltpu.VMEM((EDGE, D), BF16),
            pltpu.VMEM((7 * D, D), F32),
            pltpu.SemaphoreType.DMA((13,)), pltpu.SemaphoreType.DMA((20,)),
        ],
        compiler_params=pltpu.CompilerParams(vmem_limit_bytes=63 * 2**20),
        name="widen",
    )(fa, fo, fb, fc, vec, new_nodes, node_grad, edge_grad)


def body(
    node_states, edge_states, senders, receivers, live_count, send_rows, node_cotangent,
    edge_inner, edge_inbias, edge_outer, edge_outbias, edge_gain,
    node_inner, node_inbias, node_outer, node_outbias, node_gain,
):
    hbm = pl.BlockSpec(memory_space=pl.ANY)
    vm = pl.BlockSpec(memory_space=pltpu.VMEM)
    sm = pl.BlockSpec(memory_space=pltpu.SMEM)

    def row(v):
        return v.reshape(1, D)

    def v(shape, dtype=BF16):
        return pltpu.VMEM(shape, dtype)

    outs = pl.pallas_call(
        layer,
        out_shape=[
            jax.ShapeDtypeStruct((NODE, D), BF16),
            jax.ShapeDtypeStruct((NODE, D), BF16),
            jax.ShapeDtypeStruct((EDGE, D), BF16),
        ]
        + [jax.ShapeDtypeStruct(fin_shape(*f), BF16) for f in FINS]
        + [jax.ShapeDtypeStruct((8, D), F32)],
        in_specs=[
            hbm, hbm, vm, vm, sm, vm, hbm,
            hbm, vm, hbm, vm, vm, hbm, vm, hbm, vm, vm,
        ],
        out_specs=[hbm] * 8,
        scratch_shapes=[
            v((NODE, D)), v((EDGE, D)), v((NODE, D)),
            v((3 * D, D)), v((D, D)), v((2 * D, D)), v((D, D)),
            v((EDGE, TABLE)), v((WIDE, EDGE)), v((EDGE, NODE)), v((D, EDGE)),
            v((EDGE, D), F32), v((EDGE, D)), v((EDGE, D)), v((EDGE, 1), F32),
            v((EDGE, D)), v((EDGE, D)), v((3, PART, D), F32),
            v((WIDE, D)), v((NODE, D)), v((WIDE, D)),
            v((8, SLOT, D)), v((8, SLOT, D)), v((8, SLOT, D)), v((8, SLOT, D)),
            v((NODE, PEER)),
            v((NODE, D)), v((NODE, D), F32), v((NODE, D)), v((NODE, D)),
            v((NODE, D), F32), v((D, D), F32),
            v((NODE, D), F32), v((NODE, D), F32), v((NODE, D)), v((NODE, D)), v((NODE, D)),
            v((6, 8, D), F32),
        ]
        + [reduce_bufs(*f) for f in FINS]
        + [
            v((5, 8, D), F32), v((10, 8, D), F32),
            pltpu.SemaphoreType.DMA((7,)), pltpu.SemaphoreType.DMA((11,)),
            pltpu.SemaphoreType.DMA((16,)), pltpu.SemaphoreType.DMA((16,)),
            sem_pair(47), sem_pair(47), sem_pair(47), sem_pair(47), sem_pair(10),
        ],
        compiler_params=pltpu.CompilerParams(
            collective_id=0, has_side_effects=True, vmem_limit_bytes=63 * 2**20
        ),
        name="layer",
    )(
        node_states, edge_states, senders.reshape(16, LANE), receivers.reshape(16, LANE),
        live_count, send_rows, node_cotangent,
        edge_inner, row(edge_inbias), edge_outer, row(edge_outbias), row(edge_gain),
        node_inner, row(node_inbias), node_outer, row(node_outbias), row(node_gain),
    )
    new_nodes, node_grad, edge_grad, ei, eo, ni, no, *vecs = unpack(outs)
    vecs = [x.reshape(D) for x in vecs]
    return (
        new_nodes, node_grad, edge_grad,
        ei, vecs[0], eo, vecs[1], vecs[2],
        ni, vecs[3], no, vecs[4], vecs[5],
    )


def solution(mesh):
    nodes = P(("lat", "lon"), None)
    flat = P(("lat", "lon"))
    return jax.shard_map(
        body,
        mesh=mesh,
        in_specs=(nodes, nodes, flat, flat, flat, nodes, nodes) + (P(),) * 10,
        out_specs=(nodes, nodes, nodes) + (P(),) * 10,
        check_vma=False,
    )
```

time: 95.7 us -> 81 us (0.85)
  Pallas kernels: 91.1 us -> 79.3 us
  local copies, waits for them, and re-layouts: 2.92 us -> 0 us
    pallas_call x1, Pallas kernels: 83.5 us -> 71.9 us  [body(): pl.pallas_call(layer, out_shape=[jax.ShapeDtypeStruct((NODE, D), BF16), j...]
    unnamed x9 -> x0, local copies, waits for them, and re-layouts: 2.92 us -> none
where the time goes in v1:
time: 81 us; the launch traced here: 80.7 us
  Pallas kernels  79.3 us (98%)
  between operations  1.47 us (2%)
    pallas_call x1, Pallas kernels, body(): pl.pallas_call(layer, out_shape=[jax.ShapeDtypeStruct((NODE, D), BF16), j...  71.9 us
    pallas_call x1, Pallas kernels, unpack(): pl.pallas_call(widen, out_shape=[jax.ShapeDtypeStruct(s, t) for s, t in s...  7.4 us

profile of v1, /device:TPU:1, one launch (start us, length us, event | category | flops | bytes accessed | tf_op | source)
XLA Modules:
  0.0 80.7 jit_solution(4014478519787381998)
XLA Ops:
  1.3 71.9 %layer.1 = (bf16[512,512]{1,0:T(8,128)(2,1)}, bf16[512,512]{1,0:T(8,128)(2,1)}, bf16[2048,512]{1,0:T(8,128)(2,1)}, bf16[2,3,4,4,16,512]{5,4,3,2,1,0:T(8,128)(2,1...) custom-call(bf16[512,512]{1,0:T(8,128)(2,1)} %nodes_h.1, ...), custom_call_target="tpu_custom_call" | custom-call | tf_op jit(solution)/shard_map/layer/pallas_call | solution.py:740
  73.2 7.4 %widen.1 = (bf16[512,512]{1,0:T(8,128)(2,1)}, bf16[512,512]{1,0:T(8,128)(2,1)}, bf16[2048,512]{1,0:T(8,128)(2,1)}, f32[1536,512]{1,0:T(8,128)}, f32[512,512]{1,0...) custom-call(bf16[2,3,4,4,16,512]{5,4,3,2,1,0:T(8,128)(2,1)} %get-tup, ...), custom_call_target="tpu_custom_call" | custom-call | tf_op jit(solution)/shard_map/widen/pallas_call | solution.py:710

commit v2 on v1

--- a/solution.py
+++ b/solution.py
@@ -22,7 +22,10 @@
 WIDE = TABLE + NODE
 CHUNK = 512
 STEPS = EDGE // CHUNK
-PART = 256
+PART = 512
+NPART = 256
+NSUBS = NPART // 32
+TALL = NODE + PEER + NODE + D
 PARTS = EDGE // PART
 SUB = 32
 SUBS = PART // SUB
@@ -264,14 +267,14 @@
 def layer(
     nodes_h, edges_h, senders, receivers, live, send_rows, cot_h,
     wei_h, eib, weo_h, eob, egain, wni_h, nib, wno_h, nob, ngain,
-    new_nodes_h, node_grad_h, edge_grad_h, fin_a_h, fin_o_h, fin_b_h, fin_c_h, vec_h,
+    new_nodes_h, node_grad_h, edge_grad_h, fin_a_h, fin_b_h, fin_c_h, vec_h,
     nodes, edges, cot, wei, weo, wni, wno,
-    ohs, oht, ohr, edges_t, pre, hid, normed, scale, prnd, staging, post,
+    ohs, oht, ohr, pre, hid, normed, scale, prnd, staging, post,
     table, grad_rows, zb, halo_out, halo_in, back_out, back_in, sendt,
     new_nodes, node_base, node_grad, summed, sum_acc, outer_acc,
     npre, npost, nhid, npost_round, npre_round, acc,
-    bufs_a, bufs_o, bufs_b, bufs_c, vec, vec_slots,
-    in_sem, out_sem, halo_send, halo_recv, sems_a, sems_o, sems_b, sems_c, sems_v,
+    bufs_a, bufs_b, bufs_c, vec, vec_slots,
+    in_sem, out_sem, halo_send, halo_recv, sems_a, sems_b, sems_c, sems_v,
 ):
     place = Place()
     prd = ohs
@@ -304,8 +307,7 @@
 
     thirds = (slice(0, 1), slice(1, 2), slice(2, 3))
     red_a = Reduce(place, thirds, *bufs_a, *sems_a)
-    red_o = Reduce(place, (slice(0, 2), slice(2, 3), slice(3, 4)), *bufs_o, *sems_o)
-    red_b = Reduce(place, thirds, *bufs_b, *sems_b)
+    red_b = Reduce(place, (slice(0, 2), slice(2, 4), slice(4, 5)), *bufs_b, *sems_b)
     red_c = Reduce(place, thirds, *bufs_c, *sems_c)
     red_v = Vectors(place, vec, vec_slots, *sems_v)
 
@@ -349,7 +351,7 @@
         base = pl.multiple_of(c * CHUNK, CHUNK)
         rows = pl.ds(base, CHUNK)
         pre[rows, :] = dot(edges[rows, :], wei[0:D, :]) + eib[...]
-        edges_t[:, rows] = jnp.transpose(edges[rows, :])
+        oht[WIDE:TALL, rows] = jnp.transpose(edges[rows, :])
         for j in range(CHUNK // LANE):
             s_row = senders[pl.ds(c * (CHUNK // LANE) + j, 1), :]
             r_row = receivers[pl.ds(c * (CHUNK // LANE) + j, 1), :]
@@ -432,19 +434,25 @@
     def fold(x):
         return jnp.sum(x.reshape(x.shape[0] // 8, 8, x.shape[1]), axis=0)
 
+    def half(t):
+        return slice(t * NPART, (t + 1) * NPART)
+
+    def strip(t, s):
+        return slice(t * NPART + s * SUB, t * NPART + (s + 1) * SUB)
+
     halves = (0, 1)
     for t in halves:
-        npre[whole(t), :] += dot(summed[whole(t), :], wni[D : 2 * D, :])
+        npre[half(t), :] += dot(summed[half(t), :], wni[D : 2 * D, :])
     for t in halves:
-        for s in range(SUBS):
-            rows = part(t, s)
+        for s in range(NSUBS):
+            rows = strip(t, s)
             h, slope = silu_parts(npre[rows, :])
             nhid[rows, :] = h.astype(BF16)
             npre[rows, :] = slope
-        npost[whole(t), :] = dot(nhid[whole(t), :], wno[...])
+        npost[half(t), :] = dot(nhid[half(t), :], wno[...])
     for t in halves:
-        for s in range(SUBS):
-            rows = part(t, s)
+        for s in range(NSUBS):
+            rows = strip(t, s)
             unit, inv = normalize(npost[rows, :] + nob[...])
             new_nodes[rows, :] = (nodes[rows, :].astype(F32) + unit * ngain[...]).astype(BF16)
             cotangent = cot[rows, :].astype(F32)
@@ -452,11 +460,11 @@
             grad = norm_back(cotangent * ngain[...], unit, inv)
             acc[4] += fold(grad)
             npost_round[rows, :] = grad.astype(BF16)
-        grad = dot_rt(npost_round[whole(t), :], wno[...]) * npre[whole(t), :]
+        grad = dot_rt(npost_round[half(t), :], wno[...]) * npre[half(t), :]
         acc[3] += fold(grad)
-        npre_round[whole(t), :] = grad.astype(BF16)
+        npre_round[half(t), :] = grad.astype(BF16)
     for t in halves:
-        grad_rows[whole(t), :] = dot_rt(npre_round[whole(t), :], wni[D : 2 * D, :]).astype(BF16)
+        grad_rows[half(t), :] = dot_rt(npre_round[half(t), :], wni[D : 2 * D, :]).astype(BF16)
     s_nodes = store(0, new_nodes, new_nodes_h)
 
     def bwd_gather(t):
@@ -473,46 +481,39 @@
             prnd[rows, :] = grad.astype(BF16)
 
     def bwd_outer(t):
-        rows = slice((t - 1) * PART, (t + 1) * PART)
-        got = dot_lt(hid[rows, :], prnd[rows, :])
-        if t == 1:
+        got = dot_lt(hid[whole(t), :], prnd[whole(t), :])
+        if t == 0:
             outer_acc[...] = got
         else:
             outer_acc[...] += got
 
-    for t in range(PARTS + 1):
+    for t in range(PARTS + 2):
         at(bwd_gather, t)
+        if t == 0:
+            node_outer = dot_lt(nhid[...], npost_round[...])
+            red_a.pack(2, node_outer)
+            red_a.pack(0, dot_lt(nodes[...], npre_round[...]))
+            red_a.pack(1, dot_lt(summed[...], npre_round[...]))
         at(bwd_norm, t - 1)
         if t == 1:
-            red_a.pack(2, dot_lt(nhid[...], npost_round[...]))
+            red_a.step(0)
         if t == 2:
-            red_a.pack(0, dot_lt(nodes[...], npre_round[...]))
-        if t == 3:
-            red_a.pack(1, dot_lt(summed[...], npre_round[...]))
-            red_a.step(0)
-        if t == 4:
             node_base[...] = cot[...].astype(F32) + dot_rt(npre_round[...], wni[0:D, :])
-        if t >= 4 and t % 2 == 0:
-            bwd_outer(t - 3)
+        at(bwd_outer, t - 2)
+    left, right = slice(0, D // 2), slice(D // 2, D)
+    red_b.pack(3, outer_acc[:, left])
+    red_b.pack(4, outer_acc[:, right])
     red_a.step(1)
-    bwd_outer(PARTS - 1)
-    for j in range(4):
-        red_o.pack(j, outer_acc[:, j * LANE : (j + 1) * LANE])
-    red_o.step(0)
 
     def bwd_inner(t, cols):
         grad = dot_rt(prnd[whole(t), :], weo[cols, :]) * pre[whole(t), cols]
         acc[0, :, cols] += fold(grad)
         prd[whole(t), cols] = grad.astype(BF16)
 
-    left, right = slice(0, D // 2), slice(D // 2, D)
-    for t in range(PARTS):
-        bwd_inner(t, left)
-
-    def z_rows(j, cols):
-        zb[j * PART : (j + 1) * PART, cols] = dot(
-            oht[j * PART : (j + 1) * PART, :], prd[:, cols]
-        ).astype(BF16)
+    def tall(red, cols):
+        got = dot(oht[...], prd[:, cols])
+        zb[:, cols] = got[0:WIDE].astype(BF16)
+        red.pack(0, got[WIDE:TALL])
 
     def inner_sums(red, cols):
         incoming = halo_in[...].reshape(PEER, D)
@@ -520,35 +521,28 @@
         red.pack(2, dot_lt(nodes[...], zb[TABLE:WIDE, cols]))
         red.step(0)
 
-    for j in range(WIDE // PART):
-        z_rows(j, left)
-        bwd_inner(j, right)
-    for t in range(WIDE // PART, PARTS):
+    for t in range(PARTS):
+        bwd_inner(t, left)
+    tall(red_b, left)
+    for t in range(PARTS):
         bwd_inner(t, right)
-    red_b.pack(0, dot(edges_t[...], prd[:, left]))
     inner_sums(red_b, left)
     red_a.step(2)
-    red_o.step(1)
     vec[0, 0:6, :] = jnp.sum(acc[...], axis=1)
     vec[0, 6:8, :] = jnp.zeros((2, D), F32)
     red_v.start(0)
-    for j in range(WIDE // PART):
-        z_rows(j, right)
+    tall(red_c, right)
     red_b.step(1)
-    red_c.pack(0, dot(edges_t[...], prd[:, right]))
     inner_sums(red_c, right)
     red_a.step(3)
-    red_o.step(2)
     red_v.finish(0)
     red_v.start(1)
 
     back = dot_rt(zb[NODE:TABLE, :], wei[D : 2 * D, :]).astype(BF16)
     back_out[...] = back.reshape(8, SLOT, D)
     returning = exchange(back_out, back_in, 8)
+    red_c.step(1)
     red_a.step(4)
-    red_c.step(1)
-    red_o.step(3)
-    red_b.step(2)
     stores = []
 
     def edge_out(c):
@@ -559,24 +553,22 @@
         stores.append(store(2 + c, staging.at[rows], edge_grad_h.at[rows]))
 
     edge_out(0)
+    red_b.step(2)
+    red_c.step(2)
     red_v.finish(1)
     red_v.start(2)
     red_a.step(5)
+    edge_out(1)
     red_b.step(3)
-    red_o.step(4)
-    red_c.step(2)
-    edge_out(1)
-    red_b.step(4)
-    red_o.step(5)
     red_c.step(3)
     edge_out(2)
+    red_b.step(4)
+    red_c.step(4)
     red_v.finish(2)
     red_v.start(3)
+    red_a.step(6)
+    edge_out(3)
     red_b.step(5)
-    red_c.step(4)
-    red_o.step(6)
-    edge_out(3)
-    red_a.step(6)
     red_c.step(5)
     node_base[...] += dot_rt(zb[0:NODE, :], wei[D : 2 * D, :])
     node_base[...] += dot_rt(zb[TABLE:WIDE, :], wei[2 * D : 3 * D, :])
@@ -587,19 +579,17 @@
     stores.append(store(1, node_grad, node_grad_h))
     red_v.finish(3)
     stores.append(store(6, vec.at[4], vec_h))
-    red_b.step(6)
-    red_o.step(7)
-    stores.append(store(8, red_o.fin, fin_o_h))
     red_a.step(7)
     stores.append(store(7, red_a.fin, fin_a_h))
+    red_b.step(6)
     red_c.step(6)
     red_b.step(7)
-    stores.append(store(9, red_b.fin, fin_b_h))
+    stores.append(store(8, red_b.fin, fin_b_h))
     red_c.step(7)
-    stores.append(store(10, red_c.fin, fin_c_h))
+    stores.append(store(9, red_c.fin, fin_c_h))
     for c in halo + returning:
         c.wait_send()
-    for red in (red_a, red_o, red_b, red_c, red_v):
+    for red in (red_a, red_b, red_c, red_v):
         red.drain()
     s_nodes.wait()
     for c in stores:
@@ -610,7 +600,7 @@
     return (2, nb, 4, 4, 16, width)
 
 
-FINS = ((3, D), (4, LANE), (3, D // 2), (3, D // 2))
+FINS = ((3, D), (5, D // 2), (3, D // 2))
 
 
 def reduce_bufs(nb, width):
@@ -633,10 +623,10 @@
 
 
 def widen(
-    fa, fo, fb, fc, vec, new_nodes, node_grad, edge_grad,
+    fa, fb, fc, vec, new_nodes, node_grad, edge_grad,
     new_nodes_o, node_grad_o, edge_grad_o, edge_inner, edge_outer, node_inner, node_outer,
     v0, v1, v2, v3, v4, v5,
-    va, vo, vb, vc, vn, vg, ve, wide, in_sem, out_sem,
+    va, vb, vc, vn, vg, ve, wide, in_sem, out_sem,
 ):
     outs = []
 
@@ -653,7 +643,6 @@
     c_a = [load(h, fa.at[h], va.at[h]) for h in range(2)]
     c_b = [load(2 + h, fb.at[h], vb.at[h]) for h in range(2)]
     c_c = [load(4 + h, fc.at[h], vc.at[h]) for h in range(2)]
-    c_o = load(6, fo, vo)
     c_e = [load(7 + k, edge_grad.at[pl.ds(k * 512, 512)], ve.at[pl.ds(k * 512, 512)]) for k in range(4)]
     c_n = load(11, new_nodes, vn)
     c_g = load(12, node_grad, vg)
@@ -677,11 +666,10 @@
             wide[rows, HALF:D] = vc[h, j].reshape(HALF, HALF).astype(F32)
             store(k_out, wide.at[rows], edge_inner.at[pl.ds(j * 512 + h * HALF, HALF)])
             k_out += 1
-    c_o.wait()
     for h in range(2):
         rows = pl.ds(3072 + h * HALF, HALF)
-        for j in range(4):
-            wide[rows, j * LANE : (j + 1) * LANE] = vo[h, j].reshape(HALF, LANE).astype(F32)
+        for j in range(2):
+            wide[rows, j * HALF : (j + 1) * HALF] = vb[h, 3 + j].reshape(HALF, HALF).astype(F32)
         store(k_out, wide.at[rows], edge_outer.at[pl.ds(h * HALF, HALF)])
         k_out += 1
     for k in range(4):
@@ -699,7 +687,7 @@
 
 
 def unpack(outs):
-    new_nodes, node_grad, edge_grad, fa, fo, fb, fc, vec = outs
+    new_nodes, node_grad, edge_grad, fa, fb, fc, vec = outs
     hbm = pl.BlockSpec(memory_space=pl.ANY)
     vm = pl.BlockSpec(memory_space=pltpu.VMEM)
     shapes = [
@@ -710,7 +698,7 @@
     return pl.pallas_call(
         widen,
         out_shape=[jax.ShapeDtypeStruct(s, t) for s, t in shapes],
-        in_specs=[hbm] * 4 + [vm] + [hbm] * 3,
+        in_specs=[hbm] * 3 + [vm] + [hbm] * 3,
         out_specs=[hbm] * 7 + [vm] * 6,
         scratch_shapes=scratch + [
             pltpu.VMEM((NODE, D), BF16), pltpu.VMEM((NODE, D), BF16), pltpu.VMEM((EDGE, D), BF16),
@@ -719,7 +707,7 @@
         ],
         compiler_params=pltpu.CompilerParams(vmem_limit_bytes=63 * 2**20),
         name="widen",
-    )(fa, fo, fb, fc, vec, new_nodes, node_grad, edge_grad)
+    )(fa, fb, fc, vec, new_nodes, node_grad, edge_grad)
 
 
 def body(
@@ -750,11 +738,11 @@
             hbm, hbm, vm, vm, sm, vm, hbm,
             hbm, vm, hbm, vm, vm, hbm, vm, hbm, vm, vm,
         ],
-        out_specs=[hbm] * 8,
+        out_specs=[hbm] * 7,
         scratch_shapes=[
             v((NODE, D)), v((EDGE, D)), v((NODE, D)),
             v((3 * D, D)), v((D, D)), v((2 * D, D)), v((D, D)),
-            v((EDGE, TABLE)), v((WIDE, EDGE)), v((EDGE, NODE)), v((D, EDGE)),
+            v((EDGE, TABLE)), v((TALL, EDGE)), v((EDGE, NODE)),
             v((EDGE, D), F32), v((EDGE, D)), v((EDGE, D)), v((EDGE, 1), F32),
             v((EDGE, D)), v((EDGE, D)), v((3, PART, D), F32),
             v((WIDE, D)), v((NODE, D)), v((WIDE, D)),
@@ -770,7 +758,7 @@
             v((5, 8, D), F32), v((10, 8, D), F32),
             pltpu.SemaphoreType.DMA((7,)), pltpu.SemaphoreType.DMA((11,)),
             pltpu.SemaphoreType.DMA((16,)), pltpu.SemaphoreType.DMA((16,)),
-            sem_pair(47), sem_pair(47), sem_pair(47), sem_pair(47), sem_pair(10),
+            sem_pair(47), sem_pair(47), sem_pair(47), sem_pair(10),
         ],
         compiler_params=pltpu.CompilerParams(
             collective_id=0, has_side_effects=True, vmem_limit_bytes=63 * 2**20

time: 81 us -> 79.1 us (0.977)
  Pallas kernels: 79.3 us -> 77.4 us
    pallas_call x1, Pallas kernels: 71.9 us -> 70 us  [body(): pl.pallas_call(layer, out_shape=[jax.ShapeDtypeStruct((NODE, D), BF16), j...]
where the time goes in v2:
time: 79.1 us; the launch traced here: 78.8 us
  Pallas kernels  77.4 us (98%)
  between operations  1.47 us (2%)
    pallas_call x1, Pallas kernels, body(): pl.pallas_call(layer, out_shape=[jax.ShapeDtypeStruct((NODE, D), BF16), j...  70 us
    pallas_call x1, Pallas kernels, unpack(): pl.pallas_call(widen, out_shape=[jax.ShapeDtypeStruct(s, t) for s, t in s...  7.4 us

profile of v2, /device:TPU:1, one launch (start us, length us, event | category | flops | bytes accessed | tf_op | source)
XLA Modules:
  0.0 78.8 jit_solution(16133321409450615765)
XLA Ops:
  1.3 70.0 %layer.1 = (bf16[512,512]{1,0:T(8,128)(2,1)}, bf16[512,512]{1,0:T(8,128)(2,1)}, bf16[2048,512]{1,0:T(8,128)(2,1)}, bf16[2,3,4,4,16,512]{5,4,3,2,1,0:T(8,128)(2,1...) custom-call(bf16[512,512]{1,0:T(8,128)(2,1)} %nodes_h.1, ...), custom_call_target="tpu_custom_call" | custom-call | tf_op jit(solution)/shard_map/layer/pallas_call | solution.py:728
  71.3 7.4 %widen.1 = (bf16[512,512]{1,0:T(8,128)(2,1)}, bf16[512,512]{1,0:T(8,128)(2,1)}, bf16[2048,512]{1,0:T(8,128)(2,1)}, f32[1536,512]{1,0:T(8,128)}, f32[512,512]{1,0...) custom-call(bf16[2,3,4,4,16,512]{5,4,3,2,1,0:T(8,128)(2,1)} %get-tup, ...), custom_call_target="tpu_custom_call" | custom-call | tf_op jit(solution)/shard_map/widen/pallas_call | solution.py:698

commit v3 on v2

--- a/solution.py
+++ b/solution.py
@@ -122,28 +122,29 @@
 
 
 class Reduce:
-    def __init__(self, place, streams, gb, rc, s0, r1, s1, r2, s2, r3, fin, send, recv):
+    def __init__(self, place, streams, gb, rc, s0, q1, t1, r1, s1, r2, s2, r3, fin, send, recv):
         self.p, self.streams = place, streams
-        self.gb, self.rc, self.s0, self.r1, self.s1 = gb, rc, s0, r1, s1
-        self.r2, self.s2, self.r3, self.fin = r2, s2, r3, fin
+        self.gb, self.rc, self.s0, self.q1, self.t1 = gb, rc, s0, q1, t1
+        self.r1, self.s1, self.r2, self.s2, self.r3, self.fin = r1, s1, r2, s2, r3, fin
         self.send, self.recv = send, recv
         self.copies = {}
+        self.used = 0
 
     def pack(self, j, val):
         width = val.shape[1]
         self.gb[:, j] = val.astype(BF16).reshape(2, 4, 4, 16, width)
 
-    def copy(self, step, k, src, dst, device):
-        at = 1 + (step - 1) * 9 + k if 1 <= step <= 5 else (0 if step == 0 else 46)
+    def copy(self, step, src, dst, device):
         c = pltpu.make_async_remote_copy(
             src_ref=src,
             dst_ref=dst,
-            send_sem=self.send.at[at],
-            recv_sem=self.recv.at[at],
+            send_sem=self.send.at[self.used],
+            recv_sem=self.recv.at[self.used],
             device_id=device,
             device_id_type=MESH,
         )
         c.start()
+        self.used += 1
         self.copies.setdefault(step, []).append(c)
 
     def wait(self, step):
@@ -155,36 +156,54 @@
             axis = self.p.axis(n, level)
             for d in (2, 1, 3):
                 there = lax.rem(self.p.index(axis) + d, 4)
-                self.copy(
-                    step, n * 3 + d - 1, src(n, part, there), dst(n, part, d), self.p.shifted(axis, d)
-                )
+                self.copy(step, src(n, part, there), dst(n, part, d), self.p.shifted(axis, d))
 
     def step(self, k):
         h = self.p.core
         count = len(self.streams)
-        own = [self.p.index(self.p.axis(n, 0)) for n in range(count)]
+        ring = [self.p.axis(n, 0) for n in range(count)]
+        own = [self.p.index(axis) for axis in ring]
+        ahead = [[lax.rem(i + d, 4) for d in range(4)] for i in own]
         own2 = [self.p.index(self.p.axis(n, 1)) for n in range(count)]
+        low, high = slice(0, 2), slice(2, 4)
         if k == 0:
-            self.copy(0, 0, self.gb.at[1 - h], self.rc, self.p.twin())
+            self.copy(0, self.gb.at[1 - h], self.rc, self.p.twin())
         elif k == 1:
             self.wait(0)
             for part in self.streams:
                 mine = self.gb[h, part].astype(F32)
                 self.s0[part] = (mine + self.rc[part].astype(F32)).astype(BF16)
-            self.spread(
-                1, 0, lambda n, part, i: self.s0.at[part, i], lambda n, part, d: self.r1.at[d - 1, part]
-            )
+            for n, part in enumerate(self.streams):
+                up, down = self.p.shifted(ring[n], 1), self.p.shifted(ring[n], 3)
+                _, one, two, three = ahead[n]
+                self.copy("up", self.s0.at[part, two, low], self.q1.at[0, part], up)
+                self.copy("down", self.s0.at[part, two, high], self.q1.at[1, part], down)
+                self.copy(1, self.s0.at[part, one, high], self.r1.at[0, part], up)
+                self.copy(1, self.s0.at[part, three, low], self.r1.at[1, part], down)
         elif k == 2:
+            self.wait("up")
+            self.wait("down")
+            for n, part in enumerate(self.streams):
+                up, down = self.p.shifted(ring[n], 1), self.p.shifted(ring[n], 3)
+                _, one, _, three = ahead[n]
+                mine = self.s0[part, one, low].astype(F32)
+                self.t1[0, part] = (mine + self.q1[0, part].astype(F32)).astype(BF16)
+                mine = self.s0[part, three, high].astype(F32)
+                self.t1[1, part] = (mine + self.q1[1, part].astype(F32)).astype(BF16)
+                self.copy(1, self.t1.at[0, part], self.r1.at[2, part], up)
+                self.copy(1, self.t1.at[1, part], self.r1.at[3, part], down)
+        elif k == 3:
             self.wait(1)
             for n, part in enumerate(self.streams):
-                total = self.s0[part, own[n]].astype(F32)
-                for d in range(3):
-                    total += self.r1[d, part].astype(F32)
-                self.s1[part] = total.astype(BF16)
+                for cut, first, second in ((low, 1, 2), (high, 0, 3)):
+                    total = self.s0[part, own[n], cut].astype(F32)
+                    total += self.r1[first, part].astype(F32)
+                    total += self.r1[second, part].astype(F32)
+                    self.s1[part, cut] = total.astype(BF16)
             self.spread(
                 2, 1, lambda n, part, i: self.s1.at[part, i], lambda n, part, d: self.r2.at[d - 1, part]
             )
-        elif k == 3:
+        elif k == 4:
             self.wait(2)
             for n, part in enumerate(self.streams):
                 total = self.s1[part, own2[n]].astype(F32)
@@ -194,7 +213,7 @@
             self.spread(
                 3, 2, lambda n, part, i: self.s2.at[part], lambda n, part, d: self.r3.at[d - 1, part]
             )
-        elif k == 4:
+        elif k == 5:
             self.wait(3)
             for n, part in enumerate(self.streams):
                 near = self.s2[part].astype(F32) + self.r3[1, part].astype(F32)
@@ -205,18 +224,25 @@
                 return self.fin.at[h, part, own[n], own2[n]]
 
             self.spread(4, 1, piece, piece)
-        elif k == 5:
+        elif k == 6:
             self.wait(4)
-
-            def piece(n, part, _):
-                return self.fin.at[h, part, own[n]]
-
-            self.spread(5, 0, piece, piece)
-        elif k == 6:
+            for n, part in enumerate(self.streams):
+                piece = self.fin.at[h, part, own[n]]
+                self.copy(5, piece, piece, self.p.shifted(ring[n], 1))
+                self.copy(5, piece, piece, self.p.shifted(ring[n], 3))
+        elif k == 7:
             self.wait(5)
-            self.copy(6, 0, self.fin.at[h], self.fin.at[h], self.p.twin())
-        elif k == 7:
+            for n, part in enumerate(self.streams):
+                _, one, _, three = ahead[n]
+                piece = self.fin.at[h, part, three, low]
+                self.copy(6, piece, piece, self.p.shifted(ring[n], 1))
+                piece = self.fin.at[h, part, one, high]
+                self.copy(6, piece, piece, self.p.shifted(ring[n], 3))
+        elif k == 8:
             self.wait(6)
+            self.copy(7, self.fin.at[h], self.fin.at[h], self.p.twin())
+        elif k == 9:
+            self.wait(7)
 
     def drain(self):
         for group in self.copies.values():
@@ -347,26 +373,27 @@
     table[TABLE:WIDE, :] = dot(nodes[...], wei[2 * D : 3 * D, :]).astype(BF16)
     c_edges.wait()
 
-    def early(c, _):
-        base = pl.multiple_of(c * CHUNK, CHUNK)
-        rows = pl.ds(base, CHUNK)
+    def early(c):
+        rows = slice(c * CHUNK, (c + 1) * CHUNK)
         pre[rows, :] = dot(edges[rows, :], wei[0:D, :]) + eib[...]
-        oht[WIDE:TALL, rows] = jnp.transpose(edges[rows, :])
-        for j in range(CHUNK // LANE):
-            s_row = senders[pl.ds(c * (CHUNK // LANE) + j, 1), :]
-            r_row = receivers[pl.ds(c * (CHUNK // LANE) + j, 1), :]
-            s_col, r_col = column_of(s_row), column_of(r_row)
-            here = pl.ds(pl.multiple_of(base + j * LANE, LANE), LANE)
+        for j in range(c * (CHUNK // LANE), (c + 1) * (CHUNK // LANE)):
+            s_col, r_col = column_of(senders[j : j + 1, :]), column_of(receivers[j : j + 1, :])
+            here = slice(j * LANE, (j + 1) * LANE)
             for k in range(TABLE // LANE):
                 ohs[here, k * LANE : (k + 1) * LANE] = hot(s_col == lanes(k * LANE))
             for k in range(NODE // LANE):
                 ohr[here, k * LANE : (k + 1) * LANE] = hot(r_col == lanes(k * LANE))
-            ids = lax.broadcasted_iota(I32, (TABLE, LANE), 0)
-            oht[0:TABLE, here] = hot(ids == s_row)
-            oht[TABLE:WIDE, here] = hot(rowi == r_row)
-        return 0
-
-    lax.fori_loop(0, STEPS, early, 0)
+            oht[TABLE:WIDE, here] = hot(rowi == receivers[j : j + 1, :])
+
+    def late(c):
+        rows = slice(c * CHUNK, (c + 1) * CHUNK)
+        oht[WIDE:TALL, rows] = jnp.transpose(edges[rows, :])
+        ids = lax.broadcasted_iota(I32, (TABLE, LANE), 0)
+        for j in range(c * (CHUNK // LANE), (c + 1) * (CHUNK // LANE)):
+            oht[0:TABLE, j * LANE : (j + 1) * LANE] = hot(ids == senders[j : j + 1, :])
+
+    for c in range(STEPS):
+        early(c)
     c_wni.wait()
     npre[...] = dot(nodes[...], wni[0:D, :]) + nib[...]
     c_weo.wait()
@@ -443,6 +470,7 @@
     halves = (0, 1)
     for t in halves:
         npre[half(t), :] += dot(summed[half(t), :], wni[D : 2 * D, :])
+        late(t)
     for t in halves:
         for s in range(NSUBS):
             rows = strip(t, s)
@@ -463,6 +491,7 @@
         grad = dot_rt(npost_round[half(t), :], wno[...]) * npre[half(t), :]
         acc[3] += fold(grad)
         npre_round[half(t), :] = grad.astype(BF16)
+        late(2 + t)
     for t in halves:
         grad_rows[half(t), :] = dot_rt(npre_round[half(t), :], wni[D : 2 * D, :]).astype(BF16)
     s_nodes = store(0, new_nodes, new_nodes_h)
@@ -490,8 +519,7 @@
     for t in range(PARTS + 2):
         at(bwd_gather, t)
         if t == 0:
-            node_outer = dot_lt(nhid[...], npost_round[...])
-            red_a.pack(2, node_outer)
+            red_a.pack(2, dot_lt(nhid[...], npost_round[...]))
             red_a.pack(0, dot_lt(nodes[...], npre_round[...]))
             red_a.pack(1, dot_lt(summed[...], npre_round[...]))
         at(bwd_norm, t - 1)
@@ -499,11 +527,13 @@
             red_a.step(0)
         if t == 2:
             node_base[...] = cot[...].astype(F32) + dot_rt(npre_round[...], wni[0:D, :])
+        if t == 3:
+            red_a.step(1)
         at(bwd_outer, t - 2)
     left, right = slice(0, D // 2), slice(D // 2, D)
     red_b.pack(3, outer_acc[:, left])
     red_b.pack(4, outer_acc[:, right])
-    red_a.step(1)
+    red_a.step(2)
 
     def bwd_inner(t, cols):
         grad = dot_rt(prnd[whole(t), :], weo[cols, :]) * pre[whole(t), cols]
@@ -523,18 +553,21 @@
 
     for t in range(PARTS):
         bwd_inner(t, left)
+    red_a.step(3)
     tall(red_b, left)
     for t in range(PARTS):
         bwd_inner(t, right)
+    red_a.step(4)
     inner_sums(red_b, left)
-    red_a.step(2)
     vec[0, 0:6, :] = jnp.sum(acc[...], axis=1)
     vec[0, 6:8, :] = jnp.zeros((2, D), F32)
     red_v.start(0)
+    red_a.step(5)
     tall(red_c, right)
     red_b.step(1)
     inner_sums(red_c, right)
-    red_a.step(3)
+    red_a.step(6)
+    red_b.step(2)
     red_v.finish(0)
     red_v.start(1)
 
@@ -542,7 +575,7 @@
     back_out[...] = back.reshape(8, SLOT, D)
     returning = exchange(back_out, back_in, 8)
     red_c.step(1)
-    red_a.step(4)
+    red_b.step(3)
     stores = []
 
     def edge_out(c):
@@ -553,25 +586,26 @@
         stores.append(store(2 + c, staging.at[rows], edge_grad_h.at[rows]))
 
     edge_out(0)
-    red_b.step(2)
     red_c.step(2)
+    red_a.step(7)
+    red_b.step(4)
     red_v.finish(1)
     red_v.start(2)
-    red_a.step(5)
     edge_out(1)
-    red_b.step(3)
     red_c.step(3)
+    red_b.step(5)
+    red_a.step(8)
     edge_out(2)
-    red_b.step(4)
     red_c.step(4)
+    red_b.step(6)
     red_v.finish(2)
     red_v.start(3)
-    red_a.step(6)
     edge_out(3)
-    red_b.step(5)
     red_c.step(5)
+    red_b.step(7)
     node_base[...] += dot_rt(zb[0:NODE, :], wei[D : 2 * D, :])
     node_base[...] += dot_rt(zb[TABLE:WIDE, :], wei[2 * D : 3 * D, :])
+    red_c.step(6)
     for c in returning:
         c.wait_recv()
     owned = dot(sendt[...], back_in[...].reshape(PEER, D))
@@ -579,13 +613,14 @@
     stores.append(store(1, node_grad, node_grad_h))
     red_v.finish(3)
     stores.append(store(6, vec.at[4], vec_h))
-    red_a.step(7)
+    red_b.step(8)
+    red_a.step(9)
     stores.append(store(7, red_a.fin, fin_a_h))
-    red_b.step(6)
-    red_c.step(6)
-    red_b.step(7)
+    red_c.step(7)
+    red_b.step(9)
     stores.append(store(8, red_b.fin, fin_b_h))
-    red_c.step(7)
+    red_c.step(8)
+    red_c.step(9)
     stores.append(store(9, red_c.fin, fin_c_h))
     for c in halo + returning:
         c.wait_send()
@@ -609,7 +644,9 @@
         pltpu.VMEM(fin_shape(nb, width), BF16),
         pltpu.VMEM((nb, 4, 4) + tile, BF16),
         pltpu.VMEM((nb, 4, 4) + tile, BF16),
-        pltpu.VMEM((3, nb, 4) + tile, BF16),
+        pltpu.VMEM((2, nb, 2) + tile, BF16),
+        pltpu.VMEM((2, nb, 2) + tile, BF16),
+        pltpu.VMEM((4, nb, 2) + tile, BF16),
         pltpu.VMEM((nb, 4) + tile, BF16),
         pltpu.VMEM((3, nb) + tile, BF16),
         pltpu.VMEM((nb,) + tile, BF16),
@@ -758,7 +795,7 @@
             v((5, 8, D), F32), v((10, 8, D), F32),
             pltpu.SemaphoreType.DMA((7,)), pltpu.SemaphoreType.DMA((11,)),
             pltpu.SemaphoreType.DMA((16,)), pltpu.SemaphoreType.DMA((16,)),
-            sem_pair(47), sem_pair(47), sem_pair(47), sem_pair(10),
+            sem_pair(59), sem_pair(59), sem_pair(59), sem_pair(10),
         ],
         compiler_params=pltpu.CompilerParams(
             collective_id=0, has_side_effects=True, vmem_limit_bytes=63 * 2**20

time: 79.1 us -> 95.4 us (1.21)
  Pallas kernels: 77.4 us -> 93.6 us
    pallas_call x1, Pallas kernels: 70 us -> 86.2 us  [body(): pl.pallas_call(layer, out_shape=[jax.ShapeDtypeStruct((NODE, D), BF16), j...]
where the time goes in v3:
time: 95.4 us; the launch traced here: 95.1 us
  Pallas kernels  93.6 us (98%)
  between operations  1.49 us (2%)
    pallas_call x1, Pallas kernels, body(): pl.pallas_call(layer, out_shape=[jax.ShapeDtypeStruct((NODE, D), BF16), j...  86.2 us
    pallas_call x1, Pallas kernels, unpack(): pl.pallas_call(widen, out_shape=[jax.ShapeDtypeStruct(s, t) for s, t in s...  7.4 us

profile of v3, /device:TPU:1, one launch (start us, length us, event | category | flops | bytes accessed | tf_op | source)
XLA Modules:
  0.0 95.1 jit_solution(4500847547716195795)
XLA Ops:
  1.3 86.2 %layer.1 = (bf16[512,512]{1,0:T(8,128)(2,1)}, bf16[512,512]{1,0:T(8,128)(2,1)}, bf16[2048,512]{1,0:T(8,128)(2,1)}, bf16[2,3,4,4,16,512]{5,4,3,2,1,0:T(8,128)(2,1...) custom-call(bf16[512,512]{1,0:T(8,128)(2,1)} %nodes_h.1, ...), custom_call_target="tpu_custom_call" | custom-call | tf_op jit(solution)/shard_map/layer/pallas_call | solution.py:765
  87.5 7.4 %widen.1 = (bf16[512,512]{1,0:T(8,128)(2,1)}, bf16[512,512]{1,0:T(8,128)(2,1)}, bf16[2048,512]{1,0:T(8,128)(2,1)}, f32[1536,512]{1,0:T(8,128)}, f32[512,512]{1,0...) custom-call(bf16[2,3,4,4,16,512]{5,4,3,2,1,0:T(8,128)(2,1)} %get-tup, ...), custom_call_target="tpu_custom_call" | custom-call | tf_op jit(solution)/shard_map/widen/pallas_call | solution.py:735

commit v4 on v2

--- a/solution.py
+++ b/solution.py
@@ -91,59 +91,64 @@
         self.y = lax.div(self.lat, 2)
         self.x = lax.div(self.lon, 4)
         self.z = lax.rem(self.lon, 4)
-
-    def neighbour(self, n):
-        dlat, dlon = OFFSETS[n]
-        return (
-            lax.rem(self.lat + (dlat + N_LAT), N_LAT),
-            lax.rem(self.lon + (dlon + N_LON), N_LON),
-        )
-
-    def twin(self):
-        return (self.y * 2 + (1 - self.core), self.lon)
-
-    def index(self, axis):
-        is_x = lax.div((2 - axis) * (1 - axis), 2)
-        is_y = axis * (2 - axis)
-        is_z = lax.div(axis * (axis - 1), 2)
-        return self.x * is_x + self.y * is_y + self.z * is_z
-
-    def shifted(self, axis, d):
-        is_x = lax.div((2 - axis) * (1 - axis), 2)
-        is_y = axis * (2 - axis)
-        is_z = lax.div(axis * (axis - 1), 2)
-        x = lax.rem(self.x + d * is_x, 4)
-        y = lax.rem(self.y + d * is_y, 4)
-        z = lax.rem(self.z + d * is_z, 4)
-        return (y * 2 + self.core, x * 4 + z)
-
-    def axis(self, b, level):
-        return lax.rem(self.core + (b + level), 3)
+        self.twin = (self.lat + 1 - 2 * self.core, self.lon)
+        self.neighbour = [
+            (
+                lax.rem(self.lat + (dlat + N_LAT), N_LAT),
+                lax.rem(self.lon + (dlon + N_LON), N_LON),
+            )
+            for dlat, dlon in OFFSETS
+        ]
+        turn = [[lax.rem(i + d, 4) for d in range(4)] for i in (self.x, self.y, self.z)]
+        self.ring = [
+            [(self.lat, turn[0][d] * 4 + self.z) for d in range(4)],
+            [(turn[1][d] * 2 + self.core, self.lon) for d in range(4)],
+            [(self.lat, self.x * 4 + turn[2][d]) for d in range(4)],
+        ]
+        first, second = 1 - self.core, self.core
+
+        def pick(a, b):
+            return first * a + second * b
+
+        self.index = []
+        self.peer = []
+        for a in range(3):
+            b = (a + 1) % 3
+            self.index.append([pick(turn[a][d], turn[b][d]) for d in range(4)])
+            self.peer.append(
+                [
+                    tuple(pick(m, n) for m, n in zip(self.ring[a][d], self.ring[b][d]))
+                    for d in range(4)
+                ]
+            )
 
 
 class Reduce:
-    def __init__(self, place, streams, gb, rc, s0, r1, s1, r2, s2, r3, fin, send, recv):
-        self.p, self.streams = place, streams
+    def __init__(self, place, start, gb, rc, s0, r1, s1, r2, s2, r3, fin, send, recv):
+        self.p = place
+        self.at = [place.index[(start + level) % 3] for level in range(3)]
+        self.peer = [place.peer[(start + level) % 3] for level in range(3)]
         self.gb, self.rc, self.s0, self.r1, self.s1 = gb, rc, s0, r1, s1
         self.r2, self.s2, self.r3, self.fin = r2, s2, r3, fin
         self.send, self.recv = send, recv
         self.copies = {}
+        self.used = 0
 
     def pack(self, j, val):
         width = val.shape[1]
-        self.gb[:, j] = val.astype(BF16).reshape(2, 4, 4, 16, width)
-
-    def copy(self, step, k, src, dst, device):
-        at = 1 + (step - 1) * 9 + k if 1 <= step <= 5 else (0 if step == 0 else 46)
+        self.gb[:, :, :, j] = val.astype(BF16).reshape(2, 4, 4, 16, width)
+
+    def copy(self, step, src, dst, device):
         c = pltpu.make_async_remote_copy(
             src_ref=src,
             dst_ref=dst,
-            send_sem=self.send.at[at],
-            recv_sem=self.recv.at[at],
+            send_sem=self.send.at[self.used],
+            recv_sem=self.recv.at[self.used],
             device_id=device,
             device_id_type=MESH,
         )
         c.start()
+        self.used += 1
         self.copies.setdefault(step, []).append(c)
 
     def wait(self, step):
@@ -151,70 +156,48 @@
             c.wait_recv()
 
     def spread(self, step, level, src, dst):
-        for n, part in enumerate(self.streams):
-            axis = self.p.axis(n, level)
-            for d in (2, 1, 3):
-                there = lax.rem(self.p.index(axis) + d, 4)
-                self.copy(
-                    step, n * 3 + d - 1, src(n, part, there), dst(n, part, d), self.p.shifted(axis, d)
-                )
+        for d in (2, 1, 3):
+            self.copy(step, src(self.at[level][d]), dst(d), self.peer[level][d])
 
     def step(self, k):
         h = self.p.core
-        count = len(self.streams)
-        own = [self.p.index(self.p.axis(n, 0)) for n in range(count)]
-        own2 = [self.p.index(self.p.axis(n, 1)) for n in range(count)]
+        own, own2 = self.at[0][0], self.at[1][0]
         if k == 0:
-            self.copy(0, 0, self.gb.at[1 - h], self.rc, self.p.twin())
+            self.copy(0, self.gb.at[1 - h], self.rc, self.p.twin)
         elif k == 1:
             self.wait(0)
-            for part in self.streams:
-                mine = self.gb[h, part].astype(F32)
-                self.s0[part] = (mine + self.rc[part].astype(F32)).astype(BF16)
-            self.spread(
-                1, 0, lambda n, part, i: self.s0.at[part, i], lambda n, part, d: self.r1.at[d - 1, part]
-            )
+            for i in range(4):
+                mine = self.gb[h, i].astype(F32)
+                self.s0[i] = (mine + self.rc[i].astype(F32)).astype(BF16)
+            self.spread(1, 0, lambda i: self.s0.at[i], lambda d: self.r1.at[d - 1])
         elif k == 2:
             self.wait(1)
-            for n, part in enumerate(self.streams):
-                total = self.s0[part, own[n]].astype(F32)
-                for d in range(3):
-                    total += self.r1[d, part].astype(F32)
-                self.s1[part] = total.astype(BF16)
-            self.spread(
-                2, 1, lambda n, part, i: self.s1.at[part, i], lambda n, part, d: self.r2.at[d - 1, part]
-            )
+            total = self.s0[own].astype(F32)
+            for d in range(3):
+                total += self.r1[d].astype(F32)
+            self.s1[...] = total.astype(BF16)
+            self.spread(2, 1, lambda i: self.s1.at[i], lambda d: self.r2.at[d - 1])
         elif k == 3:
             self.wait(2)
-            for n, part in enumerate(self.streams):
-                total = self.s1[part, own2[n]].astype(F32)
-                for d in range(3):
-                    total += self.r2[d, part].astype(F32)
-                self.s2[part] = total.astype(BF16)
-            self.spread(
-                3, 2, lambda n, part, i: self.s2.at[part], lambda n, part, d: self.r3.at[d - 1, part]
-            )
+            total = self.s1[own2].astype(F32)
+            for d in range(3):
+                total += self.r2[d].astype(F32)
+            self.s2[...] = total.astype(BF16)
+            self.spread(3, 2, lambda i: self.s2, lambda d: self.r3.at[d - 1])
         elif k == 4:
             self.wait(3)
-            for n, part in enumerate(self.streams):
-                near = self.s2[part].astype(F32) + self.r3[1, part].astype(F32)
-                far = self.r3[0, part].astype(F32) + self.r3[2, part].astype(F32)
-                self.fin[h, part, own[n], own2[n]] = (near + far).astype(BF16)
-
-            def piece(n, part, _):
-                return self.fin.at[h, part, own[n], own2[n]]
-
-            self.spread(4, 1, piece, piece)
+            near = self.s2[...].astype(F32) + self.r3[1].astype(F32)
+            far = self.r3[0].astype(F32) + self.r3[2].astype(F32)
+            self.fin[h, own, own2] = (near + far).astype(BF16)
+            piece = self.fin.at[h, own, own2]
+            self.spread(4, 1, lambda i: piece, lambda d: piece)
         elif k == 5:
             self.wait(4)
-
-            def piece(n, part, _):
-                return self.fin.at[h, part, own[n]]
-
-            self.spread(5, 0, piece, piece)
+            piece = self.fin.at[h, own]
+            self.spread(5, 0, lambda i: piece, lambda d: piece)
         elif k == 6:
             self.wait(5)
-            self.copy(6, 0, self.fin.at[h], self.fin.at[h], self.p.twin())
+            self.copy(6, self.fin.at[h], self.fin.at[h], self.p.twin)
         elif k == 7:
             self.wait(6)
 
@@ -231,9 +214,7 @@
 
     def start(self, k):
         axis = k - 1
-        hops = ((0, self.p.twin()),) if k == 0 else tuple(
-            (d, self.p.shifted(jnp.int32(axis), d)) for d in (1, 2, 3)
-        )
+        hops = [(0, self.p.twin)] if k == 0 else [(d, self.p.ring[axis][d]) for d in (2, 1, 3)]
         for d, device in hops:
             at = 0 if k == 0 else 3 * (k - 1) + d
             c = pltpu.make_async_remote_copy(
@@ -298,17 +279,15 @@
     c_cot = load(6, cot_h, cot)
 
     barrier = pltpu.get_barrier_semaphore()
-    partners = [place.neighbour(n) for n in range(8)] + [place.twin()]
+    partners = place.neighbour + [place.twin]
     for axis in range(3):
-        for d in (1, 2, 3):
-            partners.append(place.shifted(jnp.int32(axis), d))
+        partners += place.ring[axis][1:]
     for device in partners:
         pl.semaphore_signal(barrier, inc=1, device_id=device, device_id_type=MESH)
 
-    thirds = (slice(0, 1), slice(1, 2), slice(2, 3))
-    red_a = Reduce(place, thirds, *bufs_a, *sems_a)
-    red_b = Reduce(place, (slice(0, 2), slice(2, 4), slice(4, 5)), *bufs_b, *sems_b)
-    red_c = Reduce(place, thirds, *bufs_c, *sems_c)
+    red_a = Reduce(place, 0, *bufs_a, *sems_a)
+    red_b = Reduce(place, 2, *bufs_b, *sems_b)
+    red_c = Reduce(place, 1, *bufs_c, *sems_c)
     red_v = Vectors(place, vec, vec_slots, *sems_v)
 
     picks = []
@@ -328,7 +307,7 @@
                 dst_ref=dst.at[7 - n],
                 send_sem=halo_send.at[base + n],
                 recv_sem=halo_recv.at[base + 7 - n],
-                device_id=place.neighbour(n),
+                device_id=place.neighbour[n],
                 device_id_type=MESH,
             )
             c.start()
@@ -597,23 +576,23 @@
 
 
 def fin_shape(nb, width):
-    return (2, nb, 4, 4, 16, width)
+    return (2, 4, 4, nb, 16, width)
 
 
 FINS = ((3, D), (5, D // 2), (3, D // 2))
 
 
 def reduce_bufs(nb, width):
-    tile = (16, width)
+    tile = (nb, 16, width)
     return (
         pltpu.VMEM(fin_shape(nb, width), BF16),
-        pltpu.VMEM((nb, 4, 4) + tile, BF16),
-        pltpu.VMEM((nb, 4, 4) + tile, BF16),
-        pltpu.VMEM((3, nb, 4) + tile, BF16),
-        pltpu.VMEM((nb, 4) + tile, BF16),
-        pltpu.VMEM((3, nb) + tile, BF16),
-        pltpu.VMEM((nb,) + tile, BF16),
-        pltpu.VMEM((3, nb) + tile, BF16),
+        pltpu.VMEM((4, 4) + tile, BF16),
+        pltpu.VMEM((4, 4) + tile, BF16),
+        pltpu.VMEM((3, 4) + tile, BF16),
+        pltpu.VMEM((4,) + tile, BF16),
+        pltpu.VMEM((3,) + tile, BF16),
+        pltpu.VMEM(tile, BF16),
+        pltpu.VMEM((3,) + tile, BF16),
         pltpu.VMEM(fin_shape(nb, width), BF16),
     )
 
@@ -654,7 +633,7 @@
         c_a[h].wait()
         for j, (out, first) in enumerate(places):
             rows = pl.ds(j * 512 + h * HALF, HALF)
-            wide[rows, :] = va[h, j].reshape(HALF, D).astype(F32)
+            wide[rows, :] = va[h, :, :, j].reshape(HALF, D).astype(F32)
             store(k_out, wide.at[rows], out.at[pl.ds(first + h * HALF, HALF)])
             k_out += 1
     for h in range(2):
@@ -662,14 +641,14 @@
         c_c[h].wait()
         for j in range(3):
             rows = pl.ds(1536 + j * 512 + h * HALF, HALF)
-            wide[rows, 0:HALF] = vb[h, j].reshape(HALF, HALF).astype(F32)
-            wide[rows, HALF:D] = vc[h, j].reshape(HALF, HALF).astype(F32)
+            wide[rows, 0:HALF] = vb[h, :, :, j].reshape(HALF, HALF).astype(F32)
+            wide[rows, HALF:D] = vc[h, :, :, j].reshape(HALF, HALF).astype(F32)
             store(k_out, wide.at[rows], edge_inner.at[pl.ds(j * 512 + h * HALF, HALF)])
             k_out += 1
     for h in range(2):
         rows = pl.ds(3072 + h * HALF, HALF)
         for j in range(2):
-            wide[rows, j * HALF : (j + 1) * HALF] = vb[h, 3 + j].reshape(HALF, HALF).astype(F32)
+            wide[rows, j * HALF : (j + 1) * HALF] = vb[h, :, :, 3 + j].reshape(HALF, HALF).astype(F32)
         store(k_out, wide.at[rows], edge_outer.at[pl.ds(h * HALF, HALF)])
         k_out += 1
     for k in range(4):
@@ -758,7 +737,7 @@
             v((5, 8, D), F32), v((10, 8, D), F32),
             pltpu.SemaphoreType.DMA((7,)), pltpu.SemaphoreType.DMA((11,)),
             pltpu.SemaphoreType.DMA((16,)), pltpu.SemaphoreType.DMA((16,)),
-            sem_pair(47), sem_pair(47), sem_pair(47), sem_pair(10),
+            sem_pair(17), sem_pair(17), sem_pair(17), sem_pair(10),
         ],
         compiler_params=pltpu.CompilerParams(
             collective_id=0, has_side_effects=True, vmem_limit_bytes=63 * 2**20

time: 79.1 us -> 92.3 us (1.17)
  Pallas kernels: 77.4 us -> 90.4 us
    pallas_call x1, Pallas kernels: 70 us -> 83 us  [body(): pl.pallas_call(layer, out_shape=[jax.ShapeDtypeStruct((NODE, D), BF16), j...]
where the time goes in v4:
time: 92.3 us; the launch traced here: 91.8 us
  Pallas kernels  90.4 us (98%)
  between operations  1.47 us (2%)
    pallas_call x1, Pallas kernels, body(): pl.pallas_call(layer, out_shape=[jax.ShapeDtypeStruct((NODE, D), BF16), j...  83 us
    pallas_call x1, Pallas kernels, unpack(): pl.pallas_call(widen, out_shape=[jax.ShapeDtypeStruct(s, t) for s, t in s...  7.4 us

profile of v4, /device:TPU:1, one launch (start us, length us, event | category | flops | bytes accessed | tf_op | source)
XLA Modules:
  0.0 91.8 jit_solution(14873462720098764326)
XLA Ops:
  1.3 83.0 %layer.1 = (bf16[512,512]{1,0:T(8,128)(2,1)}, bf16[512,512]{1,0:T(8,128)(2,1)}, bf16[2048,512]{1,0:T(8,128)(2,1)}, bf16[2,4,4,3,16,512]{5,4,3,2,1,0:T(8,128)(2,1...) custom-call(bf16[512,512]{1,0:T(8,128)(2,1)} %nodes_h.1, ...), custom_call_target="tpu_custom_call" | custom-call | tf_op jit(solution)/shard_map/layer/pallas_call | solution.py:707
  84.3 7.4 %widen.1 = (bf16[512,512]{1,0:T(8,128)(2,1)}, bf16[512,512]{1,0:T(8,128)(2,1)}, bf16[2048,512]{1,0:T(8,128)(2,1)}, f32[1536,512]{1,0:T(8,128)}, f32[512,512]{1,0...) custom-call(bf16[2,4,4,3,16,512]{5,4,3,2,1,0:T(8,128)(2,1)} %get-tup, ...), custom_call_target="tpu_custom_call" | custom-call | tf_op jit(solution)/shard_map/widen/pallas_call | solution.py:677

commit v5 on v2

--- a/solution.py
+++ b/solution.py
@@ -85,40 +85,50 @@
 
 class Place:
     def __init__(self):
-        self.lat = lax.axis_index("lat")
-        self.lon = lax.axis_index("lon")
-        self.core = lax.rem(self.lat, 2)
-        self.y = lax.div(self.lat, 2)
-        self.x = lax.div(self.lon, 4)
-        self.z = lax.rem(self.lon, 4)
-
-    def neighbour(self, n):
-        dlat, dlon = OFFSETS[n]
-        return (
-            lax.rem(self.lat + (dlat + N_LAT), N_LAT),
-            lax.rem(self.lon + (dlon + N_LON), N_LON),
-        )
-
-    def twin(self):
-        return (self.y * 2 + (1 - self.core), self.lon)
-
-    def index(self, axis):
-        is_x = lax.div((2 - axis) * (1 - axis), 2)
-        is_y = axis * (2 - axis)
-        is_z = lax.div(axis * (axis - 1), 2)
-        return self.x * is_x + self.y * is_y + self.z * is_z
-
-    def shifted(self, axis, d):
-        is_x = lax.div((2 - axis) * (1 - axis), 2)
-        is_y = axis * (2 - axis)
-        is_z = lax.div(axis * (axis - 1), 2)
-        x = lax.rem(self.x + d * is_x, 4)
-        y = lax.rem(self.y + d * is_y, 4)
-        z = lax.rem(self.z + d * is_z, 4)
-        return (y * 2 + self.core, x * 4 + z)
-
-    def axis(self, b, level):
-        return lax.rem(self.core + (b + level), 3)
+        lat = lax.axis_index("lat")
+        lon = lax.axis_index("lon")
+        self.core = lax.rem(lat, 2)
+        at = (lax.div(lon, 4), lax.div(lat, 2), lax.rem(lon, 4))
+        self.twin = (lat + 1 - 2 * self.core, lon)
+        self.neighbour = [
+            (lax.rem(lat + (dlat + N_LAT), N_LAT), lax.rem(lon + (dlon + N_LON), N_LON))
+            for dlat, dlon in OFFSETS
+        ]
+        one, two = 1 - self.core, self.core
+        self.bit, mate = {}, {}
+        for a, i in enumerate(at):
+            low, upper = lax.rem(i, 2), lax.div(i, 2)
+            odd = low + upper - 2 * low * upper
+            near, far = i + 1 - 2 * low, 3 - i
+            self.bit[a, 0] = one * odd + two * upper
+            self.bit[a, 1] = one * upper + two * odd
+            mate[a, 0] = one * near + two * far
+            mate[a, 1] = one * far + two * near
+        known = {}
+
+        def device(flips):
+            if flips not in known:
+                x, y, z = [
+                    mate[a, 0] if (a, 0) in flips else mate[a, 1] if (a, 1) in flips else at[a]
+                    for a in range(3)
+                ]
+                known[flips] = (y * 2 + self.core, x * 4 + z)
+            return known[flips]
+
+        self.level = []
+        for n in range(3):
+            a, b, c = n, (n + 1) % 3, (n + 2) % 3
+            squares = (((a, 0), (b, 0)), ((c, 0), (a, 1)), ((b, 1), (c, 1)))
+            self.level.append([])
+            for p, q in squares:
+                bp, bq = self.bit[p], self.bit[q]
+                partners = {
+                    1: (2 * bp + 1 - bq, device(frozenset((q,)))),
+                    2: (2 - 2 * bp + bq, device(frozenset((p,)))),
+                    3: (2 - 2 * bp + 1 - bq, device(frozenset((p, q)))),
+                }
+                self.level[n].append((2 * bp + bq, partners))
+        self.partners = self.neighbour + [self.twin] + list(known.values())
 
 
 class Reduce:
@@ -128,22 +138,23 @@
         self.r2, self.s2, self.r3, self.fin = r2, s2, r3, fin
         self.send, self.recv = send, recv
         self.copies = {}
+        self.used = 0
 
     def pack(self, j, val):
         width = val.shape[1]
         self.gb[:, j] = val.astype(BF16).reshape(2, 4, 4, 16, width)
 
-    def copy(self, step, k, src, dst, device):
-        at = 1 + (step - 1) * 9 + k if 1 <= step <= 5 else (0 if step == 0 else 46)
+    def copy(self, step, src, dst, device):
         c = pltpu.make_async_remote_copy(
             src_ref=src,
             dst_ref=dst,
-            send_sem=self.send.at[at],
-            recv_sem=self.recv.at[at],
+            send_sem=self.send.at[self.used],
+            recv_sem=self.recv.at[self.used],
             device_id=device,
             device_id_type=MESH,
         )
         c.start()
+        self.used += 1
         self.copies.setdefault(step, []).append(c)
 
     def wait(self, step):
@@ -151,21 +162,19 @@
             c.wait_recv()
 
     def spread(self, step, level, src, dst):
-        for n, part in enumerate(self.streams):
-            axis = self.p.axis(n, level)
-            for d in (2, 1, 3):
-                there = lax.rem(self.p.index(axis) + d, 4)
-                self.copy(
-                    step, n * 3 + d - 1, src(n, part, there), dst(n, part, d), self.p.shifted(axis, d)
-                )
+        for d in (3, 1, 2):
+            for n, part in enumerate(self.streams):
+                there, device = self.p.level[n][level][1][d]
+                self.copy(step, src(n, part, there), dst(n, part, d), device)
 
     def step(self, k):
         h = self.p.core
-        count = len(self.streams)
-        own = [self.p.index(self.p.axis(n, 0)) for n in range(count)]
-        own2 = [self.p.index(self.p.axis(n, 1)) for n in range(count)]
+        own = [self.p.level[n][0][0] for n in range(3)]
+        own2 = [self.p.level[n][1][0] for n in range(3)]
+        blocks = self.gb.shape[1]
         if k == 0:
-            self.copy(0, 0, self.gb.at[1 - h], self.rc, self.p.twin())
+            for j in range(blocks):
+                self.copy(0, self.gb.at[1 - h, j], self.rc.at[j], self.p.twin)
         elif k == 1:
             self.wait(0)
             for part in self.streams:
@@ -197,8 +206,8 @@
         elif k == 4:
             self.wait(3)
             for n, part in enumerate(self.streams):
-                near = self.s2[part].astype(F32) + self.r3[1, part].astype(F32)
-                far = self.r3[0, part].astype(F32) + self.r3[2, part].astype(F32)
+                near = self.s2[part].astype(F32) + self.r3[0, part].astype(F32)
+                far = self.r3[1, part].astype(F32) + self.r3[2, part].astype(F32)
                 self.fin[h, part, own[n], own2[n]] = (near + far).astype(BF16)
 
             def piece(n, part, _):
@@ -214,7 +223,8 @@
             self.spread(5, 0, piece, piece)
         elif k == 6:
             self.wait(5)
-            self.copy(6, 0, self.fin.at[h], self.fin.at[h], self.p.twin())
+            for j in range(blocks):
+                self.copy(6, self.fin.at[h, j], self.fin.at[h, j], self.p.twin)
         elif k == 7:
             self.wait(6)
 
@@ -230,10 +240,9 @@
         self.copies = []
 
     def start(self, k):
-        axis = k - 1
-        hops = ((0, self.p.twin()),) if k == 0 else tuple(
-            (d, self.p.shifted(jnp.int32(axis), d)) for d in (1, 2, 3)
-        )
+        hops = [(0, self.p.twin)]
+        if k:
+            hops = [(d, self.p.level[0][k - 1][1][d][1]) for d in (3, 1, 2)]
         for d, device in hops:
             at = 0 if k == 0 else 3 * (k - 1) + d
             c = pltpu.make_async_remote_copy(
@@ -255,8 +264,8 @@
             self.val[1] = self.val[0] + self.slots[0]
         else:
             at = 3 * (k - 1)
-            near = self.val[k] + self.slots[at + 2]
-            far = self.slots[at + 1] + self.slots[at + 3]
+            near = self.val[k] + self.slots[at + 1]
+            far = self.slots[at + 2] + self.slots[at + 3]
             self.val[k + 1] = near + far
 
     def drain(self):
@@ -298,10 +307,7 @@
     c_cot = load(6, cot_h, cot)
 
     barrier = pltpu.get_barrier_semaphore()
-    partners = [place.neighbour(n) for n in range(8)] + [place.twin()]
-    for axis in range(3):
-        for d in (1, 2, 3):
-            partners.append(place.shifted(jnp.int32(axis), d))
+    partners = place.partners
     for device in partners:
         pl.semaphore_signal(barrier, inc=1, device_id=device, device_id_type=MESH)
 
@@ -328,7 +334,7 @@
                 dst_ref=dst.at[7 - n],
                 send_sem=halo_send.at[base + n],
                 recv_sem=halo_recv.at[base + 7 - n],
-                device_id=place.neighbour(n),
+                device_id=place.neighbour[n],
                 device_id_type=MESH,
             )
             c.start()
@@ -758,7 +764,7 @@
             v((5, 8, D), F32), v((10, 8, D), F32),
             pltpu.SemaphoreType.DMA((7,)), pltpu.SemaphoreType.DMA((11,)),
             pltpu.SemaphoreType.DMA((16,)), pltpu.SemaphoreType.DMA((16,)),
-            sem_pair(47), sem_pair(47), sem_pair(47), sem_pair(10),
+            sem_pair(51), sem_pair(55), sem_pair(51), sem_pair(10),
         ],
         compiler_params=pltpu.CompilerParams(
             collective_id=0, has_side_effects=True, vmem_limit_bytes=63 * 2**20

time: 79.1 us -> 80.7 us (1.020)
  Pallas kernels: 77.4 us -> 78.9 us
    pallas_call x1, Pallas kernels: 70 us -> 71.5 us  [body(): pl.pallas_call(layer, out_shape=[jax.ShapeDtypeStruct((NODE, D), BF16), j...]
where the time goes in v5:
time: 80.7 us; the launch traced here: 80.4 us
  Pallas kernels  78.9 us (98%)
  between operations  1.49 us (2%)
    pallas_call x1, Pallas kernels, body(): pl.pallas_call(layer, out_shape=[jax.ShapeDtypeStruct((NODE, D), BF16), j...  71.5 us
    pallas_call x1, Pallas kernels, unpack(): pl.pallas_call(widen, out_shape=[jax.ShapeDtypeStruct(s, t) for s, t in s...  7.4 us

profile of v5, /device:TPU:1, one launch (start us, length us, event | category | flops | bytes accessed | tf_op | source)
XLA Modules:
  0.0 80.4 jit_solution(15722815145471750453)
XLA Ops:
  1.3 71.5 %layer.1 = (bf16[512,512]{1,0:T(8,128)(2,1)}, bf16[512,512]{1,0:T(8,128)(2,1)}, bf16[2048,512]{1,0:T(8,128)(2,1)}, bf16[2,3,4,4,16,512]{5,4,3,2,1,0:T(8,128)(2,1...) custom-call(bf16[512,512]{1,0:T(8,128)(2,1)} %nodes_h.1, ...), custom_call_target="tpu_custom_call" | custom-call | tf_op jit(solution)/shard_map/layer/pallas_call | solution.py:734
  72.8 7.4 %widen.1 = (bf16[512,512]{1,0:T(8,128)(2,1)}, bf16[512,512]{1,0:T(8,128)(2,1)}, bf16[2048,512]{1,0:T(8,128)(2,1)}, f32[1536,512]{1,0:T(8,128)}, f32[512,512]{1,0...) custom-call(bf16[2,3,4,4,16,512]{5,4,3,2,1,0:T(8,128)(2,1)} %get-tup, ...), custom_call_target="tpu_custom_call" | custom-call | tf_op jit(solution)/shard_map/widen/pallas_call | solution.py:704
